TPU v7x, 32 devices: a whole 2x2x4 slice. The times are simulated.
32 devices in a mesh: groups: 2 (over y), space: 4 (over z), dp: 4 (over x, core).
Axes of the slice: x: 2, y: 2, z: 4, core: 2. Of those that a mesh axis runs over, the one named last changes fastest.
Arguments:
- features: bfloat16 [8, 6144, 64], P(('groups', 'dp'), 'space'), parts along dimension 0, may hold values from -6 to 6
- kernel_map: int32 [8, 27, 6144], P(('groups', 'dp'), None, 'space'), parts along dimension 0, may hold values from 0 to 2560, as said below
- child_map: int32 [8, 8, 1536], P(('groups', 'dp'), None, 'space'), parts along dimension 0, may hold values from 0 to 2048, as said below
- live_rows: int32 [8, 4], P(('groups', 'dp'), 'space'), parts along dimension 0, may hold values from 768 to 1536, as said below
- weight_first: bfloat16 [27, 64, 64], replicated, may hold values from -0.15625 to 0.15625
- weight_second: bfloat16 [27, 64, 64], replicated, may hold values from -0.15625 to 0.15625
- weight_down: bfloat16 [8, 64, 128], replicated, may hold values from -0.25 to 0.25
- out_grad: bfloat16 [8, 1536, 128], P(('groups', 'dp'), 'space'), parts along dimension 0, may hold values from -6 to 6
Outputs:
- coarse_features: bfloat16 [8, 1536, 128], P(('groups', 'dp'), 'space'), parts along dimension 0
- feature_grad: bfloat16 [8, 6144, 64], P(('groups', 'dp'), 'space'), parts along dimension 0
- grad_first: bfloat16 [54, 64, 64], P('groups'), parts along dimension 0
- grad_second: bfloat16 [54, 64, 64], P('groups'), parts along dimension 0
- grad_down: bfloat16 [16, 64, 128], P('groups'), parts along dimension 0
There are 2 independent parts, one for each index of `groups`. A program takes and returns all parts, laid end to end along the dimension named above; an argument that names none is the same for every part. Nothing has to cross between parts.
Inputs may be any that keep to these rules, and one draw needn't show every extreme that they name: `kernel_map`: entries equal to 2560 mean no input; offset 27 // 2 of a row below its device's live count reads that row itself; rows at or above the live count read nothing. `child_map`: entries equal to 2048 mean no child; child 0 is present unless it falls past the strip's end. `live_rows`: in every sample some device is full.
All inputs are finite; a program needn't handle non-finite values.
Results may differ from a plain program's by a relative error of at most 0.006.
Values may be sent and summed in bfloat16 or wider, within the bound.
No kernel may reach another device: no remote copies, remote signals or barrier semaphores. Data moves between devices by JAX's collectives and lax.ppermute only.
A program may use at most 128 MiB of HBM per device.

v0:
```python
import jax
import jax.numpy as jnp
from jax import lax
from jax.sharding import PartitionSpec as P

HALO = 512


def extended(cells, sides, width):
    for axis, dim in sides:
        count = lax.axis_size(axis)
        ends = count - 1
        head = lax.slice_in_dim(cells, 0, width, axis=dim)
        tail = lax.slice_in_dim(cells, cells.shape[dim] - width, cells.shape[dim], axis=dim)
        cells = jnp.concatenate(
            [
                lax.ppermute(tail, axis, [(i, (i + 1) % count) for i in range(ends)]),
                cells,
                lax.ppermute(head, axis, [((i + 1) % count, i) for i in range(ends)]),
            ],
            axis=dim,
        )
    return cells


def from_behind(value, axis, steps):
    count = lax.axis_size(axis)
    leading, last = (max(0, -steps), min(count, count - steps))
    return lax.ppermute(value, axis, [(source, source + steps) for source in range(leading, last)])


def silu_slope(value):
    sig = jax.nn.sigmoid(value)
    return sig * (1.0 + value * (1.0 - sig))


def contract_first(left, right):
    return lax.dot_general(
        left, right, (((0,), (0,)), ((), ())), preferred_element_type=jnp.float32
    )


def contract_last(left, right):
    return lax.dot_general(
        left, right, (((1,), (1,)), ((), ())), preferred_element_type=jnp.float32
    )


def body(
    features, kernel_map, child_map, live_rows, weight_first, weight_second, weight_down, out_grad
):
    feats = features[0]
    offsets = kernel_map[0]
    children = child_map[0]
    grad_out = out_grad[0]
    rows = feats.shape[0]
    chans = feats.shape[1]
    wide = weight_down.shape[2]
    alive = (jnp.arange(rows, dtype=jnp.int32) < live_rows[0, 0]).astype(jnp.float32)[:, None]
    spare = jnp.zeros((1, chans), jnp.bfloat16)

    def widen(field):
        window = extended(field, (("space", 0),), HALO)
        return jnp.concatenate([window, spare], axis=0)

    def collect(padded):
        return jnp.take(padded, offsets.T, axis=0).reshape(rows, -1)

    def apply_conv(padded, weights):
        return jnp.dot(
            collect(padded),
            weights.reshape(-1, weights.shape[2]),
            preferred_element_type=jnp.float32,
        )

    def conv_back(padded, d_pre, weights):
        grad_weight = contract_first(collect(padded), d_pre).reshape(weights.shape)
        total = jnp.zeros((rows + 2 * HALO + 1, chans), jnp.float32)
        for begin in range(0, weights.shape[0], 9):
            terms = jnp.einsum(
                "ro,kio->rki", d_pre, weights[begin : begin + 9], preferred_element_type=jnp.float32
            )
            total = total.at[offsets[begin : begin + 9].T.reshape(-1)].add(terms.reshape(-1, chans))
        from_next = from_behind(total[:HALO], "space", -1)
        from_prev = from_behind(total[HALO + rows : 2 * HALO + rows], "space", 1)
        own = total[HALO : HALO + rows]
        own = own.at[rows - HALO :].add(from_next)
        own = own.at[:HALO].add(from_prev)
        return (own, grad_weight)

    padded_feats = widen(feats)
    pre_first = apply_conv(padded_feats, weight_first)
    first = (jax.nn.silu(pre_first) * alive).astype(jnp.bfloat16)
    padded_first = widen(first)
    pre_second = apply_conv(padded_first, weight_second) + feats.astype(jnp.float32)
    second = (jax.nn.silu(pre_second) * alive).astype(jnp.bfloat16)
    following = from_behind(second[:HALO], "space", -1)
    padded_second = jnp.concatenate([second, following, spare], axis=0)
    taken_down = jnp.take(padded_second, children.T, axis=0).reshape(children.shape[1], -1)
    flat_down = weight_down.reshape(-1, wide)
    coarse = jnp.dot(taken_down, flat_down, preferred_element_type=jnp.float32).astype(jnp.bfloat16)
    spread = contract_last(grad_out, flat_down)
    gathered = jnp.zeros((rows + HALO + 1, chans), jnp.float32)
    gathered = gathered.at[children.T.reshape(-1)].add(spread.reshape(-1, chans))
    returned = from_behind(gathered[rows : rows + HALO], "space", 1)
    grad_second_rows = gathered[:rows].at[:HALO].add(returned)
    grad_down = contract_first(taken_down, grad_out).reshape(weight_down.shape)
    d_second = (grad_second_rows * silu_slope(pre_second) * alive).astype(jnp.bfloat16)
    grad_first_rows, grad_second = conv_back(padded_first, d_second, weight_second)
    d_first = (grad_first_rows * silu_slope(pre_first) * alive).astype(jnp.bfloat16)
    feature_rows, grad_first = conv_back(padded_feats, d_first, weight_first)
    feature_grad = (feature_rows + d_second.astype(jnp.float32)).astype(jnp.bfloat16)
    scale = float(lax.axis_size("dp") * lax.axis_size("space") * rows) ** (-0.5)
    summed = lax.psum((grad_first, grad_second, grad_down), ("space", "dp"))
    out_first = (summed[0] * scale).astype(jnp.bfloat16)
    out_second = (summed[1] * scale).astype(jnp.bfloat16)
    out_down = (summed[2] * scale).astype(jnp.bfloat16)
    return (coarse[None], feature_grad[None], out_first, out_second, out_down)


def solution(mesh):
    placed = (
        P(("groups", "dp"), "space", None),
        P(("groups", "dp"), None, "space"),
        P(("groups", "dp"), None, "space"),
        P(("groups", "dp"), "space"),
        P(),
        P(),
        P(),
        P(("groups", "dp"), "space", None),
    )
    return jax.shard_map(
        body,
        mesh=mesh,
        in_specs=placed,
        out_specs=(
            P(("groups", "dp"), "space", None),
            P(("groups", "dp"), "space", None),
            P("groups", None, None),
            P("groups", None, None),
            P("groups", None, None),
        ),
        check_vma=False,
    )
```

profile of v0, /device:TPU:0, one launch (start us, length us, event | category | flops | bytes accessed | tf_op | source)
XLA Modules:
  0.0 1120.4 jit_solution(7453221314934102488)
XLA Ops:
  8.8 5.5 collective-permute-start
  18.1 17.1 %scatter_custom_fusion = f32[2049,64]{1,0:T(8,128)S(1)} fusion(s32[3072]{0:T(1024)S(1)} %bitcast.111, f32[3072,64]{1,0:T(8,128)S(1)} %reshape.362, f32[]{:T(128)} %constant.155.clone.1), kind=kCustom, calls=%fused_computation.29 | custom fusion | flops 196608 | bytes 524548 | tf_op jit(solution)/shard_map/scatter-add | solution.py:104
  35.4 5.2 collective-permute-start.5
  49.5 83.1 %gather_fusion.1 = bf16[41472,64]{1,0:T(8,128)(2,1)} fusion(bf16[2561,64]{1,0:T(8,128)(2,1)S(1)} %copy.66, s32[41984]{0:T(1024)S(1)} %pad_clamp_fusion), kind=kCustom, calls=%fused_computation.clone | custom fusion | bytes 10782720 | tf_op jit(solution)/shard_map/jit(_take)/gather | solution.py:67
  132.6 17.6 %reshape.423 = bf16[1536,27,64]{2,1,0:T(8,128)(2,1)} reshape(bf16[41472,64]{1,0:T(8,128)(2,1)} %gather_fusion.1) | data formatting | bytes 10616832 | tf_op jit(solution)/shard_map/jit(_take)/gather | solution.py:67
  150.2 11.2 broadcast_select_fusion
  161.4 15.5 %copy.67 = bf16[1536,27,64]{0,2,1:T(8,128)(2,1)} copy(bf16[1536,27,64]{2,1,0:T(8,128)(2,1)} %broadcast_select_fusion) | data formatting | bytes 10616832 | tf_op jit(solution)/shard_map/jit(_take)/select_n | solution.py:67
  176.9 4.3 multiply_convert_fusion.5
  181.2 2.3 collective-permute-start.2
  185.4 4.8 collective-permute-done.3
  190.5 83.1 %gather_fusion.2 = bf16[41472,64]{1,0:T(8,128)(2,1)} fusion(bf16[2561,64]{1,0:T(8,128)(2,1)S(1)} %copy.70, s32[41984]{0:T(1024)S(1)} %pad_clamp_fusion), kind=kCustom, calls=%fused_computation.1.clone | custom fusion | bytes 10782720 | tf_op jit(solution)/shard_map/jit(_take)/gather | solution.py:67
  273.6 17.6 %reshape.427 = bf16[1536,27,64]{2,1,0:T(8,128)(2,1)} reshape(bf16[41472,64]{1,0:T(8,128)(2,1)} %gather_fusion.2) | data formatting | bytes 10616832 | tf_op jit(solution)/shard_map/jit(_take)/gather | solution.py:67
  291.2 11.2 broadcast_select_fusion.1
  302.4 15.5 %copy.71 = bf16[1536,27,64]{0,2,1:T(8,128)(2,1)} copy(bf16[1536,27,64]{2,1,0:T(8,128)(2,1)} %broadcast_select_fusion.1) | data formatting | bytes 10616832 | tf_op jit(solution)/shard_map/jit(_take)/select_n | solution.py:67
  318.8 3.7 multiply_convert_fusion.3
  322.6 2.4 fusion.28
  325.0 2.4 fusion.26
  327.4 2.5 fusion.24
  329.9 2.5 fusion
  332.3 10.2 copy.81
  342.5 10.7 reshape.370
  353.2 10.2 copy.83
  363.4 10.7 reshape.378
  374.1 10.2 copy.85
  384.3 10.7 reshape.386
  396.9 75.6 %scatter_custom_fusion.1 = f32[2561,64]{1,0:T(8,128)S(1)} fusion(s32[13824]{0:T(1024)} %fusion.43, f32[13824,64]{1,0:T(8,128)} %reshape.370, f32[]{:T(128)} %constant.155.clone.1), kind=kCustom, calls=%fused_computation.26 | custom fusion | flops 884736 | bytes 656128 | tf_op jit(solution)/shard_map/scatter-add | solution.py:83
  472.5 75.8 %scatter_fusion = f32[2561,64]{1,0:T(8,128)S(1)} fusion(f32[2561,64]{1,0:T(8,128)S(1)} %scatter_custom_fusion.1, s32[13824]{0:T(1024)S(1)} %fusion.44, f32[13824,64]{1,0:T(8,128)} %reshape.378), kind=kCustom, calls=%fused_computation.5 | custom fusion | flops 884736 | bytes 10672128 | tf_op jit(solution)/shard_map/scatter-add | solution.py:83
  548.3 76.1 %scatter_fusion.1 = f32[2561,64]{1,0:T(8,128)S(1)} fusion(f32[2561,64]{1,0:T(8,128)S(1)} %scatter_fusion, s32[13824]{0:T(1024)S(1)} %fusion.45, f32[13824,64]{1,0:T(8,128)} %reshape.386), kind=kCustom, calls=%fused_computation.6 | custom fusion | flops 884736 | bytes 10672128 | tf_op jit(solution)/shard_map/scatter-add | solution.py:83
  627.8 4.5 collective-permute-start.7
  632.7 9.2 gather_fusion
  642.4 1.9 fusion.13
  645.5 3.3 fusion.21
  648.7 2.4 fusion.19
  651.1 2.4 fusion.17
  653.6 10.2 copy.90
  663.8 10.7 reshape.394
  674.5 75.6 %scatter_custom_fusion.4 = f32[2561,64]{1,0:T(8,128)S(1)} fusion(s32[13824]{0:T(1024)} %fusion.43, f32[13824,64]{1,0:T(8,128)} %reshape.394, f32[]{:T(128)} %constant.155.clone.1), kind=kCustom, calls=%fused_computation.24 | custom fusion | flops 884736 | bytes 656128 | tf_op jit(solution)/shard_map/scatter-add | solution.py:83
  750.1 10.2 copy.91
  760.3 10.7 reshape.402
  771.0 10.2 copy.92
  781.2 10.7 reshape.410
  791.9 75.8 %scatter_fusion.2 = f32[2561,64]{1,0:T(8,128)S(1)} fusion(f32[2561,64]{1,0:T(8,128)S(1)} %scatter_custom_fusion.4, s32[13824]{0:T(1024)S(1)} %fusion.44, f32[13824,64]{1,0:T(8,128)} %reshape.402), kind=kCustom, calls=%fused_computation.8 | custom fusion | flops 884736 | bytes 10672128 | tf_op jit(solution)/shard_map/scatter-add | solution.py:83
  867.7 76.1 %scatter_fusion.3 = f32[2561,64]{1,0:T(8,128)S(1)} fusion(f32[2561,64]{1,0:T(8,128)S(1)} %scatter_fusion.2, s32[13824]{0:T(1024)S(1)} %fusion.45, f32[13824,64]{1,0:T(8,128)} %reshape.410), kind=kCustom, calls=%fused_computation.9 | custom fusion | flops 884736 | bytes 10672128 | tf_op jit(solution)/shard_map/scatter-add | solution.py:83
  945.4 5.0 fusion.2
  950.9 29.2 %collective-permute-start.9 = (f32[512,64]{0,1:T(8,128)S(1)}, f32[512,64]{0,1:T(8,128)S(1)}, u32[]{:S(2)}, u32[]{:S(2)}) collective-permute-start(f32[512,64]{0,1:T(8,128)S(1)} %copy.115), channel_id=1, source_target_pairs={{0,4},{4,8},{8,12},{1,5},{5,9},{9,13},{2,6},{6,10},{10,14},{3,7},{... | collective-permute-start | bytes 393224 | tf_op jit(solution)/shard_map/ppermute | solution.py:29
  980.2 2.4 collective-permute-done.9
  983.4 125.5 %all-reduce.3.cloned.1.call-done = (f32[27,64,64]{2,1,0:T(8,128)}, f32[27,64,64]{2,1,0:T(8,128)}, f32[8,64,128]{2,1,0:T(8,128)}) async-done(((f32[27,64,64]{2,1,0:T(8,128)}, f32[27,64,64]{2,1,0:T(8,128)}, f32[8,64,128]{2,1,0:T(8,128)}), (f32[27,64,64]{2,1,0:T(8,128)}, f32[27,64,64]{2,1,0:T(8,128)}, f32[8,64,128]{2,1,0:T(8,128)})) %all-reduce.3.cloned.1.call-update) | async-done | bytes 1146896 | tf_op jit(solution)/shard_map/psum | solution.py:114
  1110.5 2.6 multiply_convert_fusion
  (116 shorter events, 28.5 us)
Async XLA Ops:
  7.2 8.5 copy-start
  7.2 33.7 %copy-start.12 = (s32[1,8,384]{2,1,0:T(8,128)S(1)}, s32[1,8,384]{2,1,0:T(8,128)}, u32[]{:S(2)}) copy-start(s32[1,8,384]{2,1,0:T(8,128)} %param.22) | copy-start | bytes 36868
  7.2 33.5 %copy-start.4 = (s32[1,27,1536]{2,0,1:T(1,128)S(1)}, s32[1,27,1536]{2,0,1:T(1,128)}, u32[]{:S(2)}) copy-start(s32[1,27,1536]{2,0,1:T(1,128)} %param.21) | copy-start | bytes 497668
  7.2 1101.7 %all-reduce.3.cloned.1.call-start = ((), (), s32[]{:S(2)}) async-start(), calls=%async_computation | async-start | bytes 4063232 | tf_op jit(solution)/shard_map/psum | solution.py:114
  8.8 39.4 %collective-permute-start = (bf16[512,64]{0,1:T(8,128)(2,1)}, bf16[512,64]{0,1:T(8,128)(2,1)}, u32[]{:S(2)}, u32[]{:S(2)}) collective-permute-start(bf16[512,64]{0,1:T(8,128)(2,1)} %get-tuple-element.81), channel_id=1, source_target_pairs={{0,4},{4,8},{8,12},{1,5},{5,9},{9,13},{2,6},{6,10},{10,14},{3,7},{... | collective-permute-start | bytes 196616 | tf_op jit(solution)/shard_map/ppermute | solution.py:17
  14.4 33.9 %collective-permute-start.1 = (bf16[512,64]{0,1:T(8,128)(2,1)S(1)}, bf16[512,64]{0,1:T(8,128)(2,1)}, u32[]{:S(2)}, u32[]{:S(2)}) collective-permute-start(bf16[512,64]{0,1:T(8,128)(2,1)S(1)} %get-tuple-element.82), channel_id=1, source_target_pairs={{4,0},{8,4},{12,8},{5,1},{9,5},{13,9},{6,2},{10,6},{14,10},{7,3},{... | collective-permute-start | bytes 196616 | tf_op jit(solution)/shard_map/ppermute | solution.py:19
  35.4 282.4 %collective-permute-start.5 = (f32[512,64]{0,1:T(8,128)S(1)}, f32[512,64]{0,1:T(8,128)}, u32[]{:S(2)}, u32[]{:S(2)}) collective-permute-start(f32[512,64]{0,1:T(8,128)S(1)} %copy.107), channel_id=1, source_target_pairs={{0,4},{4,8},{8,12},{1,5},{5,9},{9,13},{2,6},{6,10},{10,14},{3,7},{... | collective-permute-start | bytes 393224 | tf_op jit(solution)/shard_map/ppermute | solution.py:29
  40.8 7.5 copy-start.5
  48.2 270.6 %copy-start.13 = (f32[1536]{0:T(1024)}, f32[1536]{0:T(1024)S(1)}, u32[]{:S(2)}) copy-start(f32[1536]{0:T(1024)S(1)} %fusion.46) | copy-start | bytes 18436
  48.3 141.9 %copy-start.10 = (bf16[1,64]{0,1:T(8,128)(2,1)}, bf16[1,64]{0,1:T(8,128)(2,1)S(1)}, u32[]{:S(2)}) copy-start(bf16[1,64]{0,1:T(8,128)(2,1)S(1)} %broadcast_in_dim.42) | copy-start | bytes 388
  161.4 15.5 %copy-start.7 = (bf16[27,64,64]{2,1,0:T(8,128)(2,1)S(1)}, bf16[27,64,64]{2,1,0:T(8,128)(2,1)}, u32[]{:S(2)}) copy-start(bf16[27,64,64]{2,1,0:T(8,128)(2,1)} %param.24) | copy-start | bytes 663556
  181.2 4.1 collective-permute-start.2
  183.5 6.7 collective-permute-start.3
  302.4 16.4 %copy-start.6 = (bf16[27,64,64]{2,1,0:T(8,128)(2,1)S(1)}, bf16[27,64,64]{2,1,0:T(8,128)(2,1)}, u32[]{:S(2)}) copy-start(bf16[27,64,64]{2,1,0:T(8,128)(2,1)} %param.25) | copy-start | bytes 663556
  322.6 7.3 copy-start.1
  322.6 7.2 slice-start
  325.0 4.8 slice-start.1
  395.6 236.7 %collective-permute-start.4 = (bf16[512,64]{0,1:T(8,128)(2,1)}, bf16[512,64]{0,1:T(8,128)(2,1)S(1)}, u32[]{:S(2)}, u32[]{:S(2)}) collective-permute-start(bf16[512,64]{0,1:T(8,128)(2,1)} %slice.222), channel_id=1, source_target_pairs={{4,0},{8,4},{12,8},{5,1},{9,5},{13,9},{6,2},{10,6},{14,10},{7,3},{... | collective-permute-start | bytes 196616 | tf_op jit(solution)/shard_map/ppermute | solution.py:29
  624.4 7.9 copy-start.11
  624.4 8.2 copy-start.3
  625.3 19.9 %collective-permute-start.6 = (f32[512,64]{0,1:T(8,128)}, f32[512,64]{0,1:T(8,128)S(1)}, u32[]{:S(2)}, u32[]{:S(2)}) collective-permute-start(f32[512,64]{0,1:T(8,128)} %copy.110), channel_id=1, source_target_pairs={{4,0},{8,4},{12,8},{5,1},{9,5},{13,9},{6,2},{10,6},{14,10},{7,3},{... | collective-permute-start | bytes 393224 | tf_op jit(solution)/shard_map/ppermute | solution.py:29
  627.0 15.4 %copy-start.15 = (pred[384,8]{0,1:T(8,128)(4,1)S(1)}, pred[384,8]{0,1:T(8,128)(4,1)}, u32[]{:S(2)}) copy-start(pred[384,8]{0,1:T(8,128)(4,1)} %compare_and_fusion.1) | copy-start | bytes 9220
  627.8 17.5 %collective-permute-start.7 = (f32[512,64]{0,1:T(8,128)}, f32[512,64]{0,1:T(8,128)S(1)}, u32[]{:S(2)}, u32[]{:S(2)}) collective-permute-start(f32[512,64]{0,1:T(8,128)} %copy.111), channel_id=1, source_target_pairs={{0,4},{4,8},{8,12},{1,5},{5,9},{9,13},{2,6},{6,10},{10,14},{3,7},{... | collective-permute-start | bytes 393224 | tf_op jit(solution)/shard_map/ppermute | solution.py:29
  632.7 12.6 %copy-start.9 = (f32[1536,64]{0,1:T(8,128)S(1)}, f32[1536,64]{0,1:T(8,128)}, u32[]{:S(2)}) copy-start(f32[1536,64]{0,1:T(8,128)} %get-tuple-element.87) | copy-start | bytes 1179652
  632.7 12.6 %copy-start.14 = (f32[1536]{0:T(1024)S(1)}, f32[1536]{0:T(1024)}, u32[]{:S(2)}) copy-start(f32[1536]{0:T(1024)} %copy-done.13) | copy-start | bytes 18436
  641.8 6.9 copy-start.8
  944.0 38.7 %copy-start.2 = (bf16[1536,64]{0,1:T(8,128)(2,1)S(1)}, bf16[1536,64]{0,1:T(8,128)(2,1)}, u32[]{:S(2)}) copy-start(bf16[1536,64]{0,1:T(8,128)(2,1)} %copy-done.1) | copy-start | bytes 589828
  944.0 36.2 %collective-permute-start.8 = (f32[512,64]{0,1:T(8,128)S(1)}, f32[512,64]{0,1:T(8,128)S(1)}, u32[]{:S(2)}, u32[]{:S(2)}) collective-permute-start(f32[512,64]{0,1:T(8,128)S(1)} %copy.114), channel_id=1, source_target_pairs={{4,0},{8,4},{12,8},{5,1},{9,5},{13,9},{6,2},{10,6},{14,10},{7,3},{... | collective-permute-start | bytes 393224 | tf_op jit(solution)/shard_map/ppermute | solution.py:29
  950.9 31.7 %collective-permute-start.9 = (f32[512,64]{0,1:T(8,128)S(1)}, f32[512,64]{0,1:T(8,128)S(1)}, u32[]{:S(2)}, u32[]{:S(2)}) collective-permute-start(f32[512,64]{0,1:T(8,128)S(1)} %copy.115), channel_id=1, source_target_pairs={{0,4},{4,8},{8,12},{1,5},{5,9},{9,13},{2,6},{6,10},{10,14},{3,7},{... | collective-permute-start | bytes 393224 | tf_op jit(solution)/shard_map/ppermute | solution.py:29
Sparse Core Ops, SparseCore 0:
  980.3 128.6 all-reduce.2
where the time goes:
time: 1130 us; the launch traced here: 1120 us
  other arithmetic  504 us (45%)
  local copies, waits for them, and re-layouts  379 us (34%)
  waiting for transfers between devices  133 us (12%)
  starting transfers between devices  53.5 us (5%)
  matrix products  34.8 us (3%)
  between operations  15.9 us (1%)
    scatter-add x6, other arithmetic, conv_back(): total.at[offsets[begin:begin + 9].T.reshape(-1)]  455 us
    gather x4, local copies, waits for them, and re-layouts, collect(): return jnp.take(padded, offsets.T, axis=0).reshape(rows, -1)  201 us
    psum x1, waiting for transfers between devices, body(): summed = lax.psum((grad_first, grad_second, grad_down), ('space', 'dp'))  126 us
    reshape x6, local copies, waits for them, and re-layouts, conv_back(): terms.reshape(-1, chans)  64.2 us
    dot_general x6, local copies, waits for them, and re-layouts, conv_back(): jnp.einsum('ro,kio->rki', d_pre, weights[begin:begin + 9], preferred_elem...  61.2 us
    ppermute x6, starting transfers between devices, from_behind(): lax.ppermute(value, axis, [(source, source + steps) for source in range(l...  42.9 us
    select_n x3, local copies, waits for them, and re-layouts, collect(): return jnp.take(padded, offsets.T, axis=0).reshape(rows, -1)  31.3 us
  transfers between devices with their start and end apart: 11, of which 4 were waited for; matrix products, arithmetic and copies ran while one was open for 48% of the time, Pallas kernels for 0%

commit v1 on v0

v1 whole, which is shorter than its diff:
```python
import functools

import jax
import jax.numpy as jnp
from jax import lax
from jax.experimental import pallas as pl
from jax.experimental.pallas import tpu as pltpu
from jax.sharding import PartitionSpec as P

HALO = 512
SLABS = 4
VMEM_BYTES = 48 * 2**20


def silu_slope(value):
    sig = jax.nn.sigmoid(value)
    return sig * (1.0 + value * (1.0 - sig))


def split_index(index, span):
    slab = sum((index >= (s * span)).astype(jnp.int32) for s in range(1, SLABS))
    return slab, index - slab * span


def one_hot(place, span):
    shape = (span, place.shape[1])
    here = jnp.broadcast_to(place, shape).astype(jnp.int16)
    return jnp.where(
        here == lax.broadcasted_iota(jnp.int16, shape, 0), jnp.bfloat16(1), jnp.bfloat16(0)
    )


def slab_diagonal(weight):
    rows, cols = weight.shape
    tiled = jnp.concatenate([jnp.concatenate([weight] * SLABS, axis=1)] * SLABS, axis=0)
    row = lax.broadcasted_iota(jnp.int32, tiled.shape, 0) // rows
    col = lax.broadcasted_iota(jnp.int32, tiled.shape, 1) // cols
    return jnp.where(row == col, tiled, jnp.zeros_like(tiled))


def fill_slabs(slabs_ref, pieces):
    chans = pieces[0].shape[0]
    span = slabs_ref.shape[1]
    slab, at = 0, 0
    for piece in pieces:
        done = 0
        while done < piece.shape[1]:
            take = min(span - at, piece.shape[1] - done)
            slabs_ref[slab * chans : (slab + 1) * chans, at : at + take] = piece[:, done : done + take]
            done, at = done + take, at + take
            if at == span:
                slab, at = slab + 1, 0


def window_of(slabs, begin, end):
    chans = slabs.shape[0] // SLABS
    span = slabs.shape[1]
    pieces = []
    while begin < end:
        slab, at = divmod(begin, span)
        take = min(span - at, end - begin)
        pieces.append(slabs[slab * chans : (slab + 1) * chans, at : at + take])
        begin += take
    return pieces[0] if len(pieces) == 1 else jnp.concatenate(pieces, axis=1)


def fold(stacked):
    chans = stacked.shape[0] // SLABS
    return sum(stacked[s * chans : (s + 1) * chans] for s in range(SLABS))


def nt(left, right):
    return lax.dot_general(
        left, right, (((1,), (1,)), ((), ())), preferred_element_type=jnp.float32
    )


def conv(map_ref, weight_ref, slabs_ref, total_ref):
    span, rows = slabs_ref.shape[1], total_ref.shape[1]
    chans = slabs_ref.shape[0] // SLABS
    owner = lax.broadcasted_iota(jnp.int32, (SLABS * chans, rows), 0) // chans
    total_ref[...] = jnp.zeros_like(total_ref)

    def step(k, carry):
        values = jnp.dot(
            slab_diagonal(weight_ref[k].T), slabs_ref[...], preferred_element_type=jnp.float32
        ).astype(jnp.bfloat16)
        slab, place = split_index(map_ref[k], span)
        read = jnp.dot(values, one_hot(place, span), preferred_element_type=jnp.float32)
        total_ref[...] += jnp.where(slab == owner, read, 0.0)
        return carry

    lax.fori_loop(0, map_ref.shape[0], step, 0)
    return fold(total_ref[...])


def conv_back(map_ref, weight_ref, slabs_ref, grad_ref, spread_ref, total_ref, weight_grad_ref):
    span = slabs_ref.shape[1]
    chans = grad_ref.shape[0]
    row = lax.broadcasted_iota(jnp.int32, (SLABS * chans, SLABS * chans), 0) // chans
    col = lax.broadcasted_iota(jnp.int32, (SLABS * chans, SLABS * chans), 1) // chans
    total_ref[...] = jnp.zeros_like(total_ref)

    def step(k, carry):
        slab, place = split_index(map_ref[k], span)
        grad = grad_ref[...]
        for s in range(SLABS):
            spread_ref[s * chans : (s + 1) * chans, :] = jnp.where(
                slab == s, grad, jnp.zeros_like(grad)
            )
        sums = nt(spread_ref[...], one_hot(place, span)).astype(jnp.bfloat16)
        total_ref[...] += jnp.dot(
            slab_diagonal(weight_ref[k]), sums, preferred_element_type=jnp.float32
        )
        pairs = fold(jnp.where(row == col, nt(slabs_ref[...], sums), 0.0))
        weight_grad_ref[k] = sum(pairs[:, s * chans : (s + 1) * chans] for s in range(SLABS))
        return carry

    lax.fori_loop(0, map_ref.shape[0], step, 0)


def live_mask(live_ref, rows):
    return lax.broadcasted_iota(jnp.int32, (1, rows), 1) < live_ref[0, 0]


def spread_kernel(child_ref, down_ref, grad_ref, own_ref, next_ref):
    kids, chans, wide = down_ref.shape
    coarse = grad_ref.shape[0]
    rows = own_ref.shape[1]
    span = (rows + HALO) // SLABS
    total = jnp.zeros((SLABS * chans, span), jnp.float32)
    terms = nt(down_ref[...].reshape(kids * chans, wide), grad_ref[...]).astype(jnp.bfloat16)
    for j in range(kids):
        slab, place = split_index(child_ref[j : j + 1, :], span)
        term = terms[j * chans : (j + 1) * chans]
        apart = jnp.concatenate(
            [jnp.where(slab == s, term, jnp.zeros_like(term)) for s in range(SLABS)], axis=0
        )
        total += nt(apart, one_hot(place, span))
    own_ref[...] = window_of(total, 0, rows)
    next_ref[...] = window_of(total, rows, rows + HALO).astype(next_ref.dtype)


def first_kernel(
    live_ref, map_ref, weight_ref, field_ref, prev_ref, next_ref, first_ref, slope_ref, slabs_ref, total_ref
):
    fill_slabs(slabs_ref, [prev_ref, field_ref, next_ref])
    pre = conv(map_ref, weight_ref, slabs_ref, total_ref)
    alive = live_mask(live_ref, pre.shape[1])
    first_ref[...] = jnp.where(alive, jax.nn.silu(pre), 0.0).astype(jnp.bfloat16)
    slope_ref[...] = jnp.where(alive, silu_slope(pre), 0.0)


def second_kernel(
    live_ref,
    map_ref,
    weight_ref,
    first_ref,
    prev_ref,
    next_ref,
    field_ref,
    rows_ref,
    returned_ref,
    second_ref,
    d_second_ref,
    own_ref,
    to_prev_ref,
    to_next_ref,
    weight_grad_ref,
    slabs_ref,
    total_ref,
    spread_ref,
    sums_ref,
):
    fill_slabs(slabs_ref, [prev_ref, first_ref, next_ref])
    pre = conv(map_ref, weight_ref, slabs_ref, total_ref) + field_ref[...].astype(jnp.float32)
    rows = pre.shape[1]
    alive = live_mask(live_ref, rows)
    second_ref[...] = jnp.where(alive, jax.nn.silu(pre), 0.0).astype(jnp.bfloat16)
    slope = jnp.where(alive, silu_slope(pre), 0.0)
    head = rows_ref[:, :HALO] + returned_ref[...].astype(jnp.float32)
    grad_rows = jnp.concatenate([head, rows_ref[:, HALO:]], axis=1)
    d_second_ref[...] = (grad_rows * slope).astype(jnp.bfloat16)
    conv_back(map_ref, weight_ref, slabs_ref, d_second_ref, spread_ref, sums_ref, weight_grad_ref)
    sums = sums_ref[...]
    own_ref[...] = window_of(sums, HALO, HALO + rows)
    to_prev_ref[...] = window_of(sums, 0, HALO).astype(to_prev_ref.dtype)
    to_next_ref[...] = window_of(sums, HALO + rows, 2 * HALO + rows).astype(to_next_ref.dtype)


def down_kernel(child_ref, down_ref, grad_ref, second_ref, next_ref, coarse_ref, grad_down_ref, slabs_ref, taken_ref):
    kids, chans, wide = down_ref.shape
    fill_slabs(slabs_ref, [second_ref, next_ref])
    span = slabs_ref.shape[1]
    owner = lax.broadcasted_iota(jnp.int32, (SLABS * chans, grad_ref.shape[0]), 0) // chans
    for j in range(kids):
        slab, place = split_index(child_ref[j : j + 1, :], span)
        read = jnp.dot(slabs_ref[...], one_hot(place, span), preferred_element_type=jnp.float32)
        taken_ref[j * chans : (j + 1) * chans, :] = fold(
            jnp.where(slab == owner, read, 0.0)
        ).astype(jnp.bfloat16)
    taken = taken_ref[...]
    flat = down_ref[...].reshape(kids * chans, wide)
    coarse_ref[...] = jnp.dot(taken.T, flat, preferred_element_type=jnp.float32).astype(jnp.bfloat16)
    grad_down_ref[...] = jnp.dot(
        taken, grad_ref[...], preferred_element_type=jnp.float32
    ).reshape(grad_down_ref.shape)


def back_kernel(
    map_ref,
    weight_ref,
    field_ref,
    prev_ref,
    next_ref,
    rows_ref,
    from_prev_ref,
    from_next_ref,
    slope_ref,
    own_ref,
    to_prev_ref,
    to_next_ref,
    weight_grad_ref,
    slabs_ref,
    grad_ref,
    spread_ref,
    sums_ref,
):
    rows = rows_ref.shape[1]
    fill_slabs(slabs_ref, [prev_ref, field_ref, next_ref])
    grad_ref[...] = (
        jnp.concatenate(
            [
                rows_ref[:, :HALO] + from_prev_ref[...].astype(jnp.float32),
                rows_ref[:, HALO : rows - HALO],
                rows_ref[:, rows - HALO :] + from_next_ref[...].astype(jnp.float32),
            ],
            axis=1,
        )
        * slope_ref[...]
    ).astype(jnp.bfloat16)
    conv_back(map_ref, weight_ref, slabs_ref, grad_ref, spread_ref, sums_ref, weight_grad_ref)
    sums = sums_ref[...]
    own_ref[...] = window_of(sums, HALO, HALO + rows)
    to_prev_ref[...] = window_of(sums, 0, HALO).astype(to_prev_ref.dtype)
    to_next_ref[...] = window_of(sums, HALO + rows, 2 * HALO + rows).astype(to_next_ref.dtype)


def shape(dims, dtype):
    return jax.ShapeDtypeStruct(dims, dtype)


def call(kernel, outs, scratch, flops, *args):
    smem = pl.BlockSpec(memory_space=pltpu.SMEM)
    vmem = pl.BlockSpec(memory_space=pltpu.VMEM)
    return pl.pallas_call(
        kernel,
        out_shape=outs,
        in_specs=[smem if a.shape == (1, 1) else vmem for a in args],
        out_specs=[vmem] * len(outs),
        scratch_shapes=scratch,
        compiler_params=pltpu.CompilerParams(vmem_limit_bytes=VMEM_BYTES),
        cost_estimate=pl.CostEstimate(flops=flops, bytes_accessed=2**20, transcendentals=0),
    )(*args)


def to_following(value):
    count = lax.axis_size("space")
    return lax.ppermute(value, "space", [(i, i + 1) for i in range(count - 1)])


def to_preceding(value):
    count = lax.axis_size("space")
    return lax.ppermute(value, "space", [(i + 1, i) for i in range(count - 1)])


def sum_over_axes(value):
    for axis in ("dp", "space"):
        count = lax.axis_size(axis)
        if count > 4:
            value = lax.psum(value, axis)
            continue
        step = 1
        while step < count:
            sent = value.astype(jnp.bfloat16)
            value = value + lax.ppermute(sent, axis, [(i, i ^ step) for i in range(count)]).astype(
                jnp.float32
            )
            step *= 2
    return value


def body(
    features, kernel_map, child_map, live_rows, weight_first, weight_second, weight_down, out_grad
):
    field = features[0].T
    chans, rows = field.shape
    offsets = kernel_map.reshape(kernel_map.shape[1], 1, rows)
    count = offsets.shape[0]
    children = child_map[0]
    kids, coarse = children.shape
    wide = weight_down.shape[2]
    grad_out = out_grad[0]
    bf16, f32 = jnp.bfloat16, jnp.float32
    span = (rows + 2 * HALO) // SLABS
    down_span = (rows + HALO) // SLABS
    stack = SLABS * chans
    conv_flops = 2 * count * stack * span * rows

    prev_field = to_following(field[:, rows - HALO :])
    next_field = to_preceding(field[:, :HALO])
    grad_rows, spread_next = call(
        spread_kernel,
        [shape((chans, rows), f32), shape((chans, HALO), bf16)],
        [],
        2 * kids * stack * down_span * coarse,
        children,
        weight_down,
        grad_out,
    )
    returned = to_following(spread_next)
    first, slope = call(
        first_kernel,
        [shape((chans, rows), bf16), shape((chans, rows), f32)],
        [pltpu.VMEM((stack, span), bf16), pltpu.VMEM((stack, rows), f32)],
        conv_flops,
        live_rows,
        offsets,
        weight_first,
        field,
        prev_field,
        next_field,
    )
    prev_first = to_following(first[:, rows - HALO :])
    next_first = to_preceding(first[:, :HALO])
    second, d_second, own, to_prev, to_next, grad_second = call(
        second_kernel,
        [
            shape((chans, rows), bf16),
            shape((chans, rows), bf16),
            shape((chans, rows), f32),
            shape((chans, HALO), bf16),
            shape((chans, HALO), bf16),
            shape((count, chans, chans), f32),
        ],
        [
            pltpu.VMEM((stack, span), bf16),
            pltpu.VMEM((stack, rows), f32),
            pltpu.VMEM((stack, rows), bf16),
            pltpu.VMEM((stack, span), f32),
        ],
        2 * conv_flops,
        live_rows,
        offsets,
        weight_second,
        first,
        prev_first,
        next_first,
        field,
        grad_rows,
        returned,
    )
    from_next = to_preceding(to_prev)
    from_prev = to_following(to_next)
    next_second = to_preceding(second[:, :HALO])
    coarse_out, grad_down = call(
        down_kernel,
        [shape((coarse, wide), bf16), shape((kids, chans, wide), f32)],
        [pltpu.VMEM((stack, down_span), bf16), pltpu.VMEM((kids * chans, coarse), bf16)],
        2 * kids * stack * down_span * coarse,
        children,
        weight_down,
        grad_out,
        second,
        next_second,
    )
    own, to_prev, to_next, grad_first = call(
        back_kernel,
        [
            shape((chans, rows), f32),
            shape((chans, HALO), bf16),
            shape((chans, HALO), bf16),
            shape((count, chans, chans), f32),
        ],
        [
            pltpu.VMEM((stack, span), bf16),
            pltpu.VMEM((chans, rows), bf16),
            pltpu.VMEM((stack, rows), bf16),
            pltpu.VMEM((stack, span), f32),
        ],
        conv_flops,
        offsets,
        weight_first,
        field,
        prev_field,
        next_field,
        own,
        from_prev,
        from_next,
        slope,
    )
    from_next = to_preceding(to_prev).astype(f32)
    from_prev = to_following(to_next).astype(f32)
    total = own + d_second.astype(f32)
    total = total.at[:, :HALO].add(from_prev)
    total = total.at[:, rows - HALO :].add(from_next)
    feature_grad = total.astype(bf16).T
    scale = float(lax.axis_size("dp") * lax.axis_size("space") * rows) ** (-0.5)
    flat = jnp.concatenate(
        [grad_second.reshape(-1, wide), grad_down.reshape(-1, wide)], axis=0
    )
    flat = (sum_over_axes(flat) * scale).astype(bf16)
    cut = grad_second.size // wide
    out_second = flat[:cut].reshape(grad_second.shape)
    out_down = flat[cut:].reshape(grad_down.shape)
    out_first = (sum_over_axes(grad_first) * scale).astype(bf16)
    return (coarse_out[None], feature_grad[None], out_first, out_second, out_down)


def solution(mesh):
    placed = (
        P(("groups", "dp"), "space", None),
        P(("groups", "dp"), None, "space"),
        P(("groups", "dp"), None, "space"),
        P(("groups", "dp"), "space"),
        P(),
        P(),
        P(),
        P(("groups", "dp"), "space", None),
    )
    return jax.shard_map(
        body,
        mesh=mesh,
        in_specs=placed,
        out_specs=(
            P(("groups", "dp"), "space", None),
            P(("groups", "dp"), "space", None),
            P("groups", None, None),
            P("groups", None, None),
            P("groups", None, None),
        ),
        check_vma=False,
    )
```

time: 1130 us -> 246 us (0.22)
  other arithmetic: 504 us -> 4.55 us
  local copies, waits for them, and re-layouts: 379 us -> 5.33 us
  Pallas kernels: 0 us -> 139 us
  waiting for transfers between devices: 133 us -> 55.4 us
  matrix products: 34.8 us -> 0 us
  between operations: 15.9 us -> 1.63 us
  starting transfers between devices: 53.5 us -> 39.5 us
    scatter-add x12 -> x2, other arithmetic: 473 us -> 0.72 us  [the longest x1 0.69 us: body(): total = total.at[:, :HALO].add(from_prev)]
    gather x6 -> x0, local copies, waits for them, and re-layouts: 211 us -> none  [the longest x4 201 us: collect(): return jnp.take(padded, offsets.T, axis=0).reshape(rows, -1)]
    pallas_call x0 -> x5, Pallas kernels: none -> 139 us  [call(): pl.pallas_call(kernel, out_shape=outs, in_specs=[smem if a.shape == (1, 1...]
    psum x1 -> x0, waiting for transfers between devices: 126 us -> none  [body(): summed = lax.psum((grad_first, grad_second, grad_down), ('space', 'dp'))]
    reshape x11 -> x2, local copies, waits for them, and re-layouts: 66.3 us -> 1.92 us  [the longest x1 0.98 us: body(): out_second = flat[:cut].reshape(grad_second.shape)]
    dot_general x6 -> x0, local copies, waits for them, and re-layouts: 61.2 us -> none  [conv_back(): jnp.einsum('ro,kio->rki', d_pre, weights[begin:begin + 9], preferred_elem...]
    ppermute x10 -> x18, waiting for transfers between devices: 7.47 us -> 55.4 us  [the longest x8 51.5 us: sum_over_axes(): lax.ppermute(sent, axis, [(i, i ^ step) for i in range(count)])]
    dot_general x13 -> x0, matrix products: 34.8 us -> none  [the longest x6 15.3 us: conv_back(): jnp.einsum('ro,kio->rki', d_pre, weights[begin:begin + 9], preferred_elem...]
  transfers between devices with their start and end apart: 11 -> 18, of which waited for: 4 -> 10; matrix products, arithmetic and copies ran while one was open for 48% -> 2% of each run, Pallas kernels for 0% -> 29%
where the time goes in v1:
time: 246 us
  Pallas kernels  139 us (57%)
  waiting for transfers between devices  55.4 us (23%)
  starting transfers between devices  39.5 us (16%)
  local copies, waits for them, and re-layouts  5.33 us (2%)
  other arithmetic  4.55 us (2%)
    pallas_call x5, Pallas kernels, call(): pl.pallas_call(kernel, out_shape=outs, in_specs=[smem if a.shape == (1, 1...  139 us
    ppermute x8, waiting for transfers between devices, sum_over_axes(): lax.ppermute(sent, axis, [(i, i ^ step) for i in range(count)])  51.5 us
    ppermute x5, starting transfers between devices, to_following(): return lax.ppermute(value, 'space', [(i, i + 1) for i in range(count - 1)])  21.8 us
    ppermute x8, starting transfers between devices, sum_over_axes(): lax.ppermute(sent, axis, [(i, i ^ step) for i in range(count)])  11.2 us
    ppermute x5, starting transfers between devices, to_preceding(): return lax.ppermute(value, 'space', [(i + 1, i) for i in range(count - 1)])  6.58 us
  transfers between devices with their start and end apart: 18, of which 10 were waited for; matrix products, arithmetic and copies ran while one was open for 2% of the time, Pallas kernels for 29%

profile of v1, /device:TPU:0, one launch (start us, length us, event | category | flops | bytes accessed | tf_op | source)
XLA Modules:
  0.0 245.5 jit_solution(11618977583050658808)
XLA Ops:
  0.7 0.9 fusion.10
  1.6 1.3 collective-permute-start.1
  2.9 5.6 %collective-permute-start = (bf16[64,512]{1,0:T(8,128)(2,1)S(1)}, bf16[64,512]{1,0:T(8,128)(2,1)S(1)}, u32[]{:S(2)}, u32[]{:S(2)}) collective-permute-start(bf16[64,512]{1,0:T(8,128)(2,1)S(1)} %get-tuple-element.64), channel_id=1, source_target_pairs={{0,4},{4,8},{8,12},{1,5},{5,9},{9,13},{2,6},{6,10},{10,14},{3,7},{... | collective-permute-start | bytes 196616 | tf_op jit(solution)/shard_map/ppermute | solution.py:269
  8.5 1.4 shard_map.120
  9.9 3.9 %collective-permute-start.4 = (bf16[64,512]{1,0:T(8,128)(2,1)S(1)}, bf16[64,512]{1,0:T(8,128)(2,1)S(1)}, u32[]{:S(2)}, u32[]{:S(2)}) collective-permute-start(bf16[64,512]{1,0:T(8,128)(2,1)S(1)} %get-tuple-element.47), channel_id=1, source_target_pairs={{0,4},{4,8},{8,12},{1,5},{5,9},{9,13},{2,6},{6,10},{10,14},{3,7},{... | collective-permute-start | bytes 196616 | tf_op jit(solution)/shard_map/ppermute | solution.py:269
  14.6 27.7 %shard_map.119 = (bf16[64,1536]{1,0:T(8,128)(2,1)S(1)}, f32[64,1536]{1,0:T(8,128)S(1)}) custom-call(s32[1,1]{1,0:T(1,128)S(6)} %copy.15.live_ref, s32[27,1,1536]{2,1,0:T(1,128)S(1)} %bitcast.22, bf16[27,64,64]{2,1,0:T(8,128)(2,1)S(1)} %copy-done.2, bf16[64,1536]{1,0:T(8,128)(2,1)S(1)} %bitcast.19, bf16[64,512]{1,0:T(8,128)(2,1)S(1)} %collective-permute-done.prev_ref, ...), custom_call_target="tpu_custom_call" | custom-call | flops 13589544960 | bytes 1048576 | tf_op jit(solution)/shard_map/pallas_call | solution.py:256
  42.3 1.3 collective-permute-start.3
  43.6 4.5 %collective-permute-start.2 = (bf16[64,512]{1,0:T(8,128)(2,1)S(1)}, bf16[64,512]{1,0:T(8,128)(2,1)S(1)}, u32[]{:S(2)}, u32[]{:S(2)}) collective-permute-start(bf16[64,512]{1,0:T(8,128)(2,1)S(1)} %get-tuple-element.62), channel_id=1, source_target_pairs={{0,4},{4,8},{8,12},{1,5},{5,9},{9,13},{2,6},{6,10},{10,14},{3,7},{... | collective-permute-start | bytes 196616 | tf_op jit(solution)/shard_map/ppermute | solution.py:269
  48.1 0.3 collective-permute-done.3.next_ref
  48.4 1.6 collective-permute-done.2.prev_ref
  50.0 67.7 %shard_map.121 = (bf16[64,1536]{1,0:T(8,128)(2,1)S(1)}, bf16[64,1536]{1,0:T(8,128)(2,1)S(1)}, f32[64,1536]{1,0:T(8,128)S(1)}, bf16[64,512]{1,0:T(8,128)(2,1)S(1)...) custom-call(s32[1,1]{1,0:T(1,128)S(6)} %copy.15.live_ref, s32[27,1,1536]{2,1,0:T(1,128)S(1)} %bitcast.23, ...), custom_call_target="tpu_custom_call" | custom-call | flops 27179089920 | bytes 1048576 | tf_op jit(solution)/shard_map/pallas_call | solution.py:256
  117.7 0.7 copy-done.7
  118.5 4.3 %collective-permute-start.6 = (bf16[64,512]{1,0:T(8,128)(2,1)S(1)}, bf16[64,512]{1,0:T(8,128)(2,1)S(1)}, u32[]{:S(2)}, u32[]{:S(2)}) collective-permute-start(bf16[64,512]{1,0:T(8,128)(2,1)S(1)} %get-tuple-element.51), channel_id=1, source_target_pairs={{0,4},{4,8},{8,12},{1,5},{5,9},{9,13},{2,6},{6,10},{10,14},{3,7},{... | collective-permute-start | bytes 196616 | tf_op jit(solution)/shard_map/ppermute | solution.py:269
  122.7 1.3 collective-permute-start.7
  124.0 0.6 compare_reduce_fusion
  124.7 1.3 collective-permute-start.5
  126.0 0.9 reshape.75
  126.9 2.0 collective-permute-done.7.from_next_ref
  128.9 1.0 copy-done.8
  129.9 40.2 %shard_map.123 = (f32[64,1536]{1,0:T(8,128)S(1)}, bf16[64,512]{1,0:T(8,128)(2,1)S(1)}, bf16[64,512]{1,0:T(8,128)(2,1)S(1)}, f32[27,64,64]{2,1,0:T(8,128)S(1)}) custom-call(s32[27,1,1536]{2,1,0:T(1,128)S(1)} %bitcast.24, bf16[27,64,64]{2,1,0:T(8,128)(2,1)S(1)} %copy-done.2, bf16[64,1536]{1,0:T(8,128)(2,1)S(1)} %bitcast.21, ...), custom_call_target="tpu_custom_call" | custom-call | flops 13589544960 | bytes 1048576 | tf_op jit(solution)/shard_map/pallas_call | solution.py:256
  170.1 3.5 %collective-permute-start.8 = (bf16[64,512]{1,0:T(8,128)(2,1)S(1)}, bf16[64,512]{1,0:T(8,128)(2,1)S(1)}, u32[]{:S(2)}, u32[]{:S(2)}) collective-permute-start(bf16[64,512]{1,0:T(8,128)(2,1)S(1)} %get-tuple-element.56), channel_id=1, source_target_pairs={{0,4},{4,8},{8,12},{1,5},{5,9},{9,13},{2,6},{6,10},{10,14},{3,7},{... | collective-permute-start | bytes 196616 | tf_op jit(solution)/shard_map/ppermute | solution.py:269
  173.6 1.4 collective-permute-start.9
  175.0 2.2 shard_map.122
  177.4 0.6 collective-permute-start.10
  178.0 1.6 collective-permute-done.10
  179.6 0.1 fusion
  179.7 1.6 collective-permute-start.11
  181.4 0.6 collective-permute-start.15
  182.0 0.7 fusion.5
  182.7 10.1 %collective-permute-done.11 = bf16[27,64,64]{2,1,0:T(8,128)(2,1)S(1)} collective-permute-done((bf16[27,64,64]{2,1,0:T(8,128)(2,1)S(1)}, bf16[27,64,64]{2,1,0:T(8,128)(2,1)S(1)}, u32[]{:S(2)}, u32[]{:S(2)}) %collective-permute-start.11) | collective-permute-done | bytes 221216 | tf_op jit(solution)/shard_map/ppermute | solution.py:286
  192.8 0.2 fusion.7
  193.0 2.7 %collective-permute-start.12 = (bf16[27,64,64]{2,1,0:T(8,128)(2,1)S(1)}, bf16[27,64,64]{2,1,0:T(8,128)(2,1)S(1)}, u32[]{:S(2)}, u32[]{:S(2)}) collective-permute-start(bf16[27,64,64]{2,1,0:T(8,128)(2,1)S(1)} %fusion.7), channel_id=1, source_target_pairs={{0,4},{4,0},{8,12},{12,8},{1,5},{5,1},{9,13},{13,9},{2,6},{6,2},{1... | collective-permute-start | bytes 663560 | tf_op jit(solution)/shard_map/ppermute | solution.py:286
  195.7 3.9 %collective-permute-done.15 = bf16[1376,128]{1,0:T(8,128)(2,1)S(1)} collective-permute-done((bf16[1376,128]{1,0:T(8,128)(2,1)S(1)}, bf16[1376,128]{1,0:T(8,128)(2,1)S(1)}, u32[]{:S(2)}, u32[]{:S(2)}) %collective-permute-start.15) | collective-permute-done | bytes 352288 | tf_op jit(solution)/shard_map/ppermute | solution.py:286
  199.6 0.1 fusion.3
  199.7 2.7 %collective-permute-start.16 = (bf16[1376,128]{1,0:T(8,128)(2,1)S(1)}, bf16[1376,128]{1,0:T(8,128)(2,1)S(1)}, u32[]{:S(2)}, u32[]{:S(2)}) collective-permute-start(bf16[1376,128]{1,0:T(8,128)(2,1)S(1)} %fusion.3), channel_id=1, source_target_pairs={{0,4},{4,0},{8,12},{12,8},{1,5},{5,1},{9,13},{13,9},{2,6},{6,2},{1... | collective-permute-start | bytes 1056776 | tf_op jit(solution)/shard_map/ppermute | solution.py:286
  202.5 8.8 %collective-permute-done.12 = bf16[27,64,64]{2,1,0:T(8,128)(2,1)S(1)} collective-permute-done((bf16[27,64,64]{2,1,0:T(8,128)(2,1)S(1)}, bf16[27,64,64]{2,1,0:T(8,128)(2,1)S(1)}, u32[]{:S(2)}, u32[]{:S(2)}) %collective-permute-start.12) | collective-permute-done | bytes 221216 | tf_op jit(solution)/shard_map/ppermute | solution.py:286
  211.2 0.3 fusion.1
  211.5 1.0 collective-permute-start.13
  212.5 4.6 %collective-permute-done.16 = bf16[1376,128]{1,0:T(8,128)(2,1)S(1)} collective-permute-done((bf16[1376,128]{1,0:T(8,128)(2,1)S(1)}, bf16[1376,128]{1,0:T(8,128)(2,1)S(1)}, u32[]{:S(2)}, u32[]{:S(2)}) %collective-permute-start.16) | collective-permute-done | bytes 352288 | tf_op jit(solution)/shard_map/ppermute | solution.py:286
  217.2 0.2 fusion.4
  217.3 1.9 collective-permute-start.17
  219.3 0.7 convert_bitcast_fusion
  220.0 19.9 %collective-permute-done.13 = bf16[27,64,64]{2,1,0:T(8,128)(2,1)S(1)} collective-permute-done((bf16[27,64,64]{2,1,0:T(8,128)(2,1)S(1)}, bf16[27,64,64]{2,1,0:T(8,128)(2,1)S(1)}, u32[]{:S(2)}, u32[]{:S(2)}) %collective-permute-start.13) | collective-permute-done | bytes 221216 | tf_op jit(solution)/shard_map/ppermute | solution.py:286
  239.8 1.1 multiply_convert_fusion
  241.0 2.7 %collective-permute-done.17 = bf16[1376,128]{1,0:T(8,128)(2,1)S(1)} collective-permute-done((bf16[1376,128]{1,0:T(8,128)(2,1)S(1)}, bf16[1376,128]{1,0:T(8,128)(2,1)S(1)}, u32[]{:S(2)}, u32[]{:S(2)}) %collective-permute-start.17) | collective-permute-done | bytes 352288 | tf_op jit(solution)/shard_map/ppermute | solution.py:286
  243.6 0.2 multiply_convert_fusion.1
  243.9 0.7 slice.73
  244.5 1.0 reshape.77
  (35 shorter events, 0.4 us)
Async XLA Ops:
  0.6 7.8 %copy-start.4 = (bf16[8,64,128]{2,1,0:T(8,128)(2,1)S(1)}, bf16[8,64,128]{2,1,0:T(8,128)(2,1)}, u32[]{:S(2)}) copy-start(bf16[8,64,128]{2,1,0:T(8,128)(2,1)} %down_ref.3) | copy-start | bytes 393220
  0.6 7.8 %copy-start.5 = (bf16[1,384,128]{2,1,0:T(8,128)(2,1)S(1)}, bf16[1,384,128]{2,1,0:T(8,128)(2,1)}, u32[]{:S(2)}) copy-start(bf16[1,384,128]{2,1,0:T(8,128)(2,1)} %param.19) | copy-start | bytes 294916
  0.7 7.8 %copy-start.6 = (s32[1,8,384]{2,1,0:T(8,128)S(1)}, s32[1,8,384]{2,1,0:T(8,128)}, u32[]{:S(2)}) copy-start(s32[1,8,384]{2,1,0:T(8,128)} %param.14) | copy-start | bytes 36868
  1.6 12.9 %collective-permute-start.1 = (bf16[64,512]{1,0:T(8,128)(2,1)S(1)}, bf16[64,512]{1,0:T(8,128)(2,1)S(1)}, u32[]{:S(2)}, u32[]{:S(2)}) collective-permute-start(bf16[64,512]{1,0:T(8,128)(2,1)S(1)} %get-tuple-element.63), channel_id=1, source_target_pairs={{4,0},{8,4},{12,8},{5,1},{9,5},{13,9},{6,2},{10,6},{14,10},{7,3},{... | collective-permute-start | bytes 196616 | tf_op jit(solution)/shard_map/ppermute | solution.py:274
  2.9 11.6 %collective-permute-start = (bf16[64,512]{1,0:T(8,128)(2,1)S(1)}, bf16[64,512]{1,0:T(8,128)(2,1)S(1)}, u32[]{:S(2)}, u32[]{:S(2)}) collective-permute-start(bf16[64,512]{1,0:T(8,128)(2,1)S(1)} %get-tuple-element.64), channel_id=1, source_target_pairs={{0,4},{4,8},{8,12},{1,5},{5,9},{9,13},{2,6},{6,10},{10,14},{3,7},{... | collective-permute-start | bytes 196616 | tf_op jit(solution)/shard_map/ppermute | solution.py:269
  8.5 6.0 %copy-start = (bf16[1,1536,64]{1,2,0:T(8,128)(2,1)S(1)}, bf16[1,1536,64]{1,2,0:T(8,128)(2,1)}, u32[]{:S(2)}) copy-start(bf16[1,1536,64]{1,2,0:T(8,128)(2,1)} %param.12) | copy-start | bytes 589828
  8.5 6.0 %copy-start.2 = (bf16[27,64,64]{2,1,0:T(8,128)(2,1)S(1)}, bf16[27,64,64]{2,1,0:T(8,128)(2,1)}, u32[]{:S(2)}) copy-start(bf16[27,64,64]{2,1,0:T(8,128)(2,1)} %weight_ref.5) | copy-start | bytes 663556
  8.5 6.0 %copy-start.3 = (s32[1,27,1536]{2,0,1:T(1,128)S(1)}, s32[1,27,1536]{2,0,1:T(1,128)}, u32[]{:S(2)}) copy-start(s32[1,27,1536]{2,0,1:T(1,128)} %param.13) | copy-start | bytes 497668
  9.9 38.2 %collective-permute-start.4 = (bf16[64,512]{1,0:T(8,128)(2,1)S(1)}, bf16[64,512]{1,0:T(8,128)(2,1)S(1)}, u32[]{:S(2)}, u32[]{:S(2)}) collective-permute-start(bf16[64,512]{1,0:T(8,128)(2,1)S(1)} %get-tuple-element.47), channel_id=1, source_target_pairs={{0,4},{4,8},{8,12},{1,5},{5,9},{9,13},{2,6},{6,10},{10,14},{3,7},{... | collective-permute-start | bytes 196616 | tf_op jit(solution)/shard_map/ppermute | solution.py:269
  14.6 35.4 %copy-start.1 = (bf16[27,64,64]{2,1,0:T(8,128)(2,1)S(1)}, bf16[27,64,64]{2,1,0:T(8,128)(2,1)}, u32[]{:S(2)}) copy-start(bf16[27,64,64]{2,1,0:T(8,128)(2,1)} %weight_ref.4) | copy-start | bytes 663556
  42.3 6.2 %collective-permute-start.3 = (bf16[64,512]{1,0:T(8,128)(2,1)S(1)}, bf16[64,512]{1,0:T(8,128)(2,1)S(1)}, u32[]{:S(2)}, u32[]{:S(2)}) collective-permute-start(bf16[64,512]{1,0:T(8,128)(2,1)S(1)} %get-tuple-element.61), channel_id=1, source_target_pairs={{4,0},{8,4},{12,8},{5,1},{9,5},{13,9},{6,2},{10,6},{14,10},{7,3},{... | collective-permute-start | bytes 196616 | tf_op jit(solution)/shard_map/ppermute | solution.py:274
  43.6 6.4 %collective-permute-start.2 = (bf16[64,512]{1,0:T(8,128)(2,1)S(1)}, bf16[64,512]{1,0:T(8,128)(2,1)S(1)}, u32[]{:S(2)}, u32[]{:S(2)}) collective-permute-start(bf16[64,512]{1,0:T(8,128)(2,1)S(1)} %get-tuple-element.62), channel_id=1, source_target_pairs={{0,4},{4,8},{8,12},{1,5},{5,9},{9,13},{2,6},{6,10},{10,14},{3,7},{... | collective-permute-start | bytes 196616 | tf_op jit(solution)/shard_map/ppermute | solution.py:269
  117.7 0.7 copy-start.7
  118.5 8.4 %collective-permute-start.6 = (bf16[64,512]{1,0:T(8,128)(2,1)S(1)}, bf16[64,512]{1,0:T(8,128)(2,1)S(1)}, u32[]{:S(2)}, u32[]{:S(2)}) collective-permute-start(bf16[64,512]{1,0:T(8,128)(2,1)S(1)} %get-tuple-element.51), channel_id=1, source_target_pairs={{0,4},{4,8},{8,12},{1,5},{5,9},{9,13},{2,6},{6,10},{10,14},{3,7},{... | collective-permute-start | bytes 196616 | tf_op jit(solution)/shard_map/ppermute | solution.py:269
  122.7 6.2 %collective-permute-start.7 = (bf16[64,512]{1,0:T(8,128)(2,1)S(1)}, bf16[64,512]{1,0:T(8,128)(2,1)S(1)}, u32[]{:S(2)}, u32[]{:S(2)}) collective-permute-start(bf16[64,512]{1,0:T(8,128)(2,1)S(1)} %get-tuple-element.52), channel_id=1, source_target_pairs={{4,0},{8,4},{12,8},{5,1},{9,5},{13,9},{6,2},{10,6},{14,10},{7,3},{... | collective-permute-start | bytes 196616 | tf_op jit(solution)/shard_map/ppermute | solution.py:274
  124.7 50.3 %collective-permute-start.5 = (bf16[64,512]{1,0:T(8,128)(2,1)S(1)}, bf16[64,512]{1,0:T(8,128)(2,1)S(1)}, u32[]{:S(2)}, u32[]{:S(2)}) collective-permute-start(bf16[64,512]{1,0:T(8,128)(2,1)S(1)} %slice.63), channel_id=1, source_target_pairs={{4,0},{8,4},{12,8},{5,1},{9,5},{13,9},{6,2},{10,6},{14,10},{7,3},{... | collective-permute-start | bytes 196616 | tf_op jit(solution)/shard_map/ppermute | solution.py:274
  128.9 1.0 copy-start.8
  170.1 11.9 %collective-permute-start.8 = (bf16[64,512]{1,0:T(8,128)(2,1)S(1)}, bf16[64,512]{1,0:T(8,128)(2,1)S(1)}, u32[]{:S(2)}, u32[]{:S(2)}) collective-permute-start(bf16[64,512]{1,0:T(8,128)(2,1)S(1)} %get-tuple-element.56), channel_id=1, source_target_pairs={{0,4},{4,8},{8,12},{1,5},{5,9},{9,13},{2,6},{6,10},{10,14},{3,7},{... | collective-permute-start | bytes 196616 | tf_op jit(solution)/shard_map/ppermute | solution.py:269
  173.6 3.6 %copy-start.9 = (f32[864,128]{1,0:T(8,128)S(1)}, f32[864,128]{1,0:T(8,128)}, u32[]{:S(2)}) copy-start(f32[864,128]{1,0:T(8,128)} %reshape.75) | copy-start | bytes 1327108
  173.6 28.9 %collective-permute-start.9 = (bf16[64,512]{1,0:T(8,128)(2,1)S(1)}, bf16[64,512]{1,0:T(8,128)(2,1)S(1)}, u32[]{:S(2)}, u32[]{:S(2)}) collective-permute-start(bf16[64,512]{1,0:T(8,128)(2,1)S(1)} %get-tuple-element.57), channel_id=1, source_target_pairs={{4,0},{8,4},{12,8},{5,1},{9,5},{13,9},{6,2},{10,6},{14,10},{7,3},{... | collective-permute-start | bytes 196616 | tf_op jit(solution)/shard_map/ppermute | solution.py:274
  177.2 4.1 %collective-permute-start.14 = (bf16[1376,128]{1,0:T(8,128)(2,1)S(1)}, bf16[1376,128]{1,0:T(8,128)(2,1)S(1)}, u32[]{:S(2)}, u32[]{:S(2)}) collective-permute-start(bf16[1376,128]{1,0:T(8,128)(2,1)S(1)} %fusion.2), channel_id=1, source_target_pairs={{0,1},{1,0},{2,3},{3,2},{4,5},{5,4},{6,7},{7,6},{8,9},{9,8},{10,11... | collective-permute-start | bytes 1056776 | tf_op jit(solution)/shard_map/ppermute | solution.py:286
  177.4 2.2 collective-permute-start.10
  179.7 13.1 %collective-permute-start.11 = (bf16[27,64,64]{2,1,0:T(8,128)(2,1)S(1)}, bf16[27,64,64]{2,1,0:T(8,128)(2,1)S(1)}, u32[]{:S(2)}, u32[]{:S(2)}) collective-permute-start(bf16[27,64,64]{2,1,0:T(8,128)(2,1)S(1)} %fusion), channel_id=1, source_target_pairs={{0,2},{1,3},{2,0},{3,1},{4,6},{5,7},{6,4},{7,5},{8,10},{9,11},{10,... | collective-permute-start | bytes 663560 | tf_op jit(solution)/shard_map/ppermute | solution.py:286
  181.4 18.2 %collective-permute-start.15 = (bf16[1376,128]{1,0:T(8,128)(2,1)S(1)}, bf16[1376,128]{1,0:T(8,128)(2,1)S(1)}, u32[]{:S(2)}, u32[]{:S(2)}) collective-permute-start(bf16[1376,128]{1,0:T(8,128)(2,1)S(1)} %fusion.8), channel_id=1, source_target_pairs={{0,2},{1,3},{2,0},{3,1},{4,6},{5,7},{6,4},{7,5},{8,10},{9,11},{10,... | collective-permute-start | bytes 1056776 | tf_op jit(solution)/shard_map/ppermute | solution.py:286
  193.0 18.2 %collective-permute-start.12 = (bf16[27,64,64]{2,1,0:T(8,128)(2,1)S(1)}, bf16[27,64,64]{2,1,0:T(8,128)(2,1)S(1)}, u32[]{:S(2)}, u32[]{:S(2)}) collective-permute-start(bf16[27,64,64]{2,1,0:T(8,128)(2,1)S(1)} %fusion.7), channel_id=1, source_target_pairs={{0,4},{4,0},{8,12},{12,8},{1,5},{5,1},{9,13},{13,9},{2,6},{6,2},{1... | collective-permute-start | bytes 663560 | tf_op jit(solution)/shard_map/ppermute | solution.py:286
  199.7 17.4 %collective-permute-start.16 = (bf16[1376,128]{1,0:T(8,128)(2,1)S(1)}, bf16[1376,128]{1,0:T(8,128)(2,1)S(1)}, u32[]{:S(2)}, u32[]{:S(2)}) collective-permute-start(bf16[1376,128]{1,0:T(8,128)(2,1)S(1)} %fusion.3), channel_id=1, source_target_pairs={{0,4},{4,0},{8,12},{12,8},{1,5},{5,1},{9,13},{13,9},{2,6},{6,2},{1... | collective-permute-start | bytes 1056776 | tf_op jit(solution)/shard_map/ppermute | solution.py:286
  211.5 28.3 %collective-permute-start.13 = (bf16[27,64,64]{2,1,0:T(8,128)(2,1)S(1)}, bf16[27,64,64]{2,1,0:T(8,128)(2,1)S(1)}, u32[]{:S(2)}, u32[]{:S(2)}) collective-permute-start(bf16[27,64,64]{2,1,0:T(8,128)(2,1)S(1)} %fusion.1), channel_id=1, source_target_pairs={{0,8},{4,12},{8,0},{12,4},{1,9},{5,13},{9,1},{13,5},{2,10},{6,14},... | collective-permute-start | bytes 663560 | tf_op jit(solution)/shard_map/ppermute | solution.py:286
  217.3 26.3 %collective-permute-start.17 = (bf16[1376,128]{1,0:T(8,128)(2,1)S(1)}, bf16[1376,128]{1,0:T(8,128)(2,1)S(1)}, u32[]{:S(2)}, u32[]{:S(2)}) collective-permute-start(bf16[1376,128]{1,0:T(8,128)(2,1)S(1)} %fusion.4), channel_id=1, source_target_pairs={{0,8},{4,12},{8,0},{12,4},{1,9},{5,13},{9,1},{13,5},{2,10},{6,14},... | collective-permute-start | bytes 1056776 | tf_op jit(solution)/shard_map/ppermute | solution.py:286

commit v2 on v0

v2 whole, which is shorter than its diff:
```python
import jax
import jax.numpy as jnp
from jax import lax
from jax.experimental import pallas as pl
from jax.experimental.pallas import tpu as pltpu
from jax.sharding import PartitionSpec as P

HALO = 512
READ_SPAN = 512
SPREAD_SPAN = 256
DOWN_SPAN = 512
UNROLL = 9
VMEM_BYTES = 40 * 2**20
LIVE, FIRST, LAST, DP = range(4)


def silu_slope(value):
    sig = jax.nn.sigmoid(value)
    return sig * (1.0 + value * (1.0 - sig))


def locate(index, span):
    slab = lax.shift_right_arithmetic(index, span.bit_length() - 1)
    return slab, jnp.where(index >= 0, index & (span - 1), -1)


def one_hot(place, span):
    shape = (span, place.shape[1])
    here = jnp.broadcast_to(place, shape).astype(jnp.int16)
    return jnp.where(
        here == lax.broadcasted_iota(jnp.int16, shape, 0), jnp.bfloat16(1), jnp.bfloat16(0)
    )


def nt(left, right):
    return lax.dot_general(
        left, right, (((1,), (1,)), ((), ())), preferred_element_type=jnp.float32
    )


def nn(left, right):
    return jnp.dot(left, right, preferred_element_type=jnp.float32)


def read_rows(slabs, index, chans):
    count, span = slabs.shape[0] // chans, slabs.shape[1]
    slab, place = locate(index, span)
    read = nn(slabs, one_hot(place, span))
    picked = read[(count - 1) * chans :]
    for s in range(count - 1):
        picked = jnp.where(slab == s, read[s * chans : (s + 1) * chans], picked)
    return picked.astype(jnp.bfloat16)


def spread_rows(terms_ref, terms, index, count, span):
    chans = terms.shape[0]
    slab, place = locate(index, span)
    for s in range(count):
        terms_ref[s * chans : (s + 1) * chans, :] = jnp.where(slab == s, terms, jnp.zeros_like(terms))
    return nt(terms_ref[...], one_hot(place, span))


def conv(map_ref, weight_ref, slabs_ref, taken_ref):
    count, chans = weight_ref.shape[0], weight_ref.shape[1]
    rows = taken_ref.shape[1]
    window = rows + 2 * HALO

    def step(k, carry):
        index = map_ref[k]
        index = jnp.where(index < window, index, -1)
        at = pl.ds(pl.multiple_of(k * chans, chans), chans)
        for begin in range(0, rows, HALO):
            part = slice(begin, begin + HALO)
            taken_ref[at, part] = read_rows(slabs_ref[...], index[:, part], chans)
        return carry

    lax.fori_loop(0, count, step, 0, unroll=UNROLL)
    weights = weight_ref[...].reshape(count * chans, -1).T
    return nn(weights, taken_ref[...])


def side_by_side(weight_ref):
    return jnp.concatenate([weight_ref[k] for k in range(weight_ref.shape[0])], axis=1)


def conv_back(map_ref, weight_ref, grad_ref, terms_ref, sums_ref, halo):
    count, chans = weight_ref.shape[0], weight_ref.shape[1]
    rows = grad_ref.shape[1]
    slabs = sums_ref.shape[0]

    def step(k, carry):
        index = map_ref[k]
        if halo:
            after = (index >= HALO + rows) & (index < 2 * HALO + rows)
            index = jnp.where(after, index - rows, jnp.where(index < HALO, index, -1))
        else:
            index = jnp.where(index < HALO + rows, index - HALO, -1)
        sums = spread_rows(terms_ref, grad_ref[...], index, slabs, SPREAD_SPAN).astype(jnp.bfloat16)
        at = pl.ds(pl.multiple_of(k * chans, chans), chans)
        for s in range(slabs):
            sums_ref[s, at, :] = sums[s * chans : (s + 1) * chans]
        return carry

    lax.fori_loop(0, count, step, 0, unroll=UNROLL)
    weights = side_by_side(weight_ref)
    return [nn(weights, sums_ref[s]) for s in range(slabs)]


def put_window(slabs_ref, info_ref, before, own_ref, after):
    chans, rows = own_ref.shape
    zero = jnp.zeros_like(before)
    slabs_ref[:chans, :] = jnp.where(info_ref[0, FIRST] == 1, zero, before)
    for s in range(rows // READ_SPAN):
        slabs_ref[(s + 1) * chans : (s + 2) * chans, :] = own_ref[:, s * READ_SPAN : (s + 1) * READ_SPAN]
    last = rows // READ_SPAN + 1
    slabs_ref[last * chans : (last + 1) * chans, :] = jnp.where(info_ref[0, LAST] == 1, zero, after)


def live_mask(info_ref, rows):
    return lax.broadcasted_iota(jnp.int32, (1, rows), 1) < info_ref[0, LIVE]


def add_ends(info_ref, rows_ref, before, after):
    rows = rows_ref.shape[1]
    before = jnp.where(info_ref[0, FIRST] == 1, 0.0, before.astype(jnp.float32))
    after = jnp.where(info_ref[0, LAST] == 1, 0.0, after.astype(jnp.float32))
    return jnp.concatenate(
        [
            rows_ref[:, :HALO] + before,
            rows_ref[:, HALO : rows - HALO],
            rows_ref[:, rows - HALO :] + after,
        ],
        axis=1,
    )


def spread_kernel(child_ref, down_ref, grad_ref, own_ref, next_ref, terms_ref):
    kids, chans, wide = down_ref.shape
    coarse = grad_ref.shape[0]
    rows = own_ref.shape[1]
    slabs = (rows + HALO) // DOWN_SPAN
    total = jnp.zeros((slabs * chans, DOWN_SPAN), jnp.float32)
    terms = nt(down_ref[...].reshape(kids * chans, wide), grad_ref[...]).astype(jnp.bfloat16)
    for j in range(kids):
        index = child_ref[j : j + 1, :]
        index = jnp.where(index < rows + HALO, index, -1)
        total += spread_rows(terms_ref, terms[j * chans : (j + 1) * chans], index, slabs, DOWN_SPAN)
    for s in range(slabs - 1):
        own_ref[:, s * DOWN_SPAN : (s + 1) * DOWN_SPAN] = total[s * chans : (s + 1) * chans]
    next_ref[...] = total[(slabs - 1) * chans :].astype(next_ref.dtype)


def first_kernel(
    info_ref,
    map_ref,
    weight_ref,
    field_ref,
    before_ref,
    after_ref,
    spread_ref,
    first_ref,
    slope_ref,
    taken_ref,
    to_next_ref,
    slabs_ref,
):
    put_window(slabs_ref, info_ref, before_ref[...], field_ref, after_ref[...])
    pre = conv(map_ref, weight_ref, slabs_ref, taken_ref)
    chans, rows = pre.shape
    alive = live_mask(info_ref, rows)
    first_ref[...] = jnp.where(alive, jax.nn.silu(pre), 0.0).astype(jnp.bfloat16)
    slope_ref[...] = jnp.where(alive, silu_slope(pre), 0.0)
    to_next_ref[:chans] = first_ref[:, rows - HALO :]
    to_next_ref[chans:] = spread_ref[...]


def second_kernel(
    info_ref,
    map_ref,
    weight_ref,
    first_ref,
    before_ref,
    after_ref,
    field_ref,
    rows_ref,
    second_ref,
    d_second_ref,
    grad_weight_ref,
    to_prev_ref,
    to_next_ref,
    slabs_ref,
    taken_ref,
    terms_ref,
    sums_ref,
):
    chans, rows = first_ref.shape
    put_window(slabs_ref, info_ref, before_ref[:chans], first_ref, after_ref[...])
    pre = conv(map_ref, weight_ref, slabs_ref, taken_ref) + field_ref[...].astype(jnp.float32)
    alive = live_mask(info_ref, rows)
    second_ref[...] = jnp.where(alive, jax.nn.silu(pre), 0.0).astype(jnp.bfloat16)
    slope = jnp.where(alive, silu_slope(pre), 0.0)
    returned = jnp.where(info_ref[0, FIRST] == 1, 0.0, before_ref[chans:].astype(jnp.float32))
    grad_rows = jnp.concatenate([rows_ref[:, :HALO] + returned, rows_ref[:, HALO:]], axis=1)
    d_second_ref[...] = (grad_rows * slope).astype(jnp.bfloat16)
    grad_weight_ref[...] = nt(d_second_ref[...], taken_ref[...])
    ends = conv_back(map_ref, weight_ref, d_second_ref, terms_ref, sums_ref, True)
    half = len(ends) // 2
    to_prev_ref[:chans] = jnp.concatenate(ends[:half], axis=1).astype(to_prev_ref.dtype)
    to_prev_ref[chans:] = second_ref[:, :HALO]
    to_next_ref[...] = jnp.concatenate(ends[half:], axis=1).astype(to_next_ref.dtype)


def own_kernel(map_ref, weight_ref, grad_ref, own_ref, terms_ref, sums_ref):
    parts = conv_back(map_ref, weight_ref, grad_ref, terms_ref, sums_ref, False)
    for s, part in enumerate(parts):
        own_ref[:, s * SPREAD_SPAN : (s + 1) * SPREAD_SPAN] = part


def ends_kernel(map_ref, weight_ref, grad_ref, to_prev_ref, to_next_ref, terms_ref, sums_ref):
    ends = conv_back(map_ref, weight_ref, grad_ref, terms_ref, sums_ref, True)
    half = len(ends) // 2
    to_prev_ref[...] = jnp.concatenate(ends[:half], axis=1).astype(to_prev_ref.dtype)
    to_next_ref[...] = jnp.concatenate(ends[half:], axis=1).astype(to_next_ref.dtype)


def middle_kernel(
    info_ref,
    child_ref,
    down_ref,
    grad_ref,
    second_ref,
    from_next_ref,
    from_prev_ref,
    rows_ref,
    slope_ref,
    taken_ref,
    grad_second_ref,
    coarse_ref,
    d_first_ref,
    grads_ref,
    slabs_ref,
    kids_ref,
):
    kids, chans, wide = down_ref.shape
    rows = second_ref.shape[1]
    for s in range(rows // DOWN_SPAN):
        slabs_ref[s * chans : (s + 1) * chans, :] = second_ref[:, s * DOWN_SPAN : (s + 1) * DOWN_SPAN]
    after = from_next_ref[chans:]
    slabs_ref[rows // DOWN_SPAN * chans :, :] = jnp.where(
        info_ref[0, LAST] == 1, jnp.zeros_like(after), after
    )
    for j in range(kids):
        index = child_ref[j : j + 1, :]
        index = jnp.where(index < rows + HALO, index, -1)
        kids_ref[j * chans : (j + 1) * chans, :] = read_rows(slabs_ref[...], index, chans)
    taken = kids_ref[...]
    flat = down_ref[...].reshape(kids * chans, wide)
    coarse_ref[...] = nn(taken.T, flat).astype(jnp.bfloat16)
    grad_down = nn(taken, grad_ref[...])
    d_first_ref[...] = (
        add_ends(info_ref, rows_ref, from_prev_ref[...], from_next_ref[:chans]) * slope_ref[...]
    ).astype(jnp.bfloat16)
    size = grad_second_ref.shape[1]
    grads_ref[:, :size] = grad_second_ref[...]
    grads_ref[:, size : 2 * size] = nt(d_first_ref[...], taken_ref[...])
    for j in range(kids):
        grads_ref[:, 2 * size + j * wide : 2 * size + (j + 1) * wide] = grad_down[
            j * chans : (j + 1) * chans
        ]


def last_kernel(info_ref, own_ref, d_second_ref, before_ref, after_ref, grads_ref, field_ref, first_ref, second_ref, down_ref):
    total = add_ends(info_ref, own_ref, before_ref[...], after_ref[...])
    field_ref[...] = (total + d_second_ref[...].astype(jnp.float32)).astype(jnp.bfloat16)
    count, chans = first_ref.shape[0], first_ref.shape[1]
    kids, wide = down_ref.shape[0], down_ref.shape[2]
    size = count * chans
    second = grads_ref[:, :size].T
    first = grads_ref[:, size : 2 * size].T
    for k in range(count):
        second_ref[k] = second[k * chans : (k + 1) * chans]
        first_ref[k] = first[k * chans : (k + 1) * chans]
    for j in range(kids):
        down_ref[j] = grads_ref[:, 2 * size + j * wide : 2 * size + (j + 1) * wide]


def shape(dims, dtype):
    return jax.ShapeDtypeStruct(dims, dtype)


def call(kernel, outs, scratch, flops, *args):
    smem = pl.BlockSpec(memory_space=pltpu.SMEM)
    vmem = pl.BlockSpec(memory_space=pltpu.VMEM)
    return pl.pallas_call(
        kernel,
        out_shape=outs,
        in_specs=[smem if a.shape == (1, 4) else vmem for a in args],
        out_specs=[vmem] * len(outs),
        scratch_shapes=scratch,
        compiler_params=pltpu.CompilerParams(vmem_limit_bytes=VMEM_BYTES),
        cost_estimate=pl.CostEstimate(flops=flops, bytes_accessed=2**20, transcendentals=0),
    )(*args)


def shifted(value, axis, steps):
    count = lax.axis_size(axis)
    return lax.ppermute(value, axis, [(i, (i + steps) % count) for i in range(count)])


def body(
    features, kernel_map, child_map, live_rows, weight_first, weight_second, weight_down, out_grad
):
    bf16, f32 = jnp.bfloat16, jnp.float32
    field = features[0].T
    chans, rows = field.shape
    count = kernel_map.shape[1]
    offsets = kernel_map.reshape(count, 1, rows)
    children = child_map[0]
    kids, coarse = children.shape
    wide = weight_down.shape[2]
    grad_out = out_grad[0]
    place = lax.axis_index("space")
    devices = lax.axis_size("space")
    info = jnp.stack(
        [
            live_rows[0, 0],
            (place == 0).astype(jnp.int32),
            (place == devices - 1).astype(jnp.int32),
            lax.axis_index("dp").astype(jnp.int32),
        ]
    ).reshape(1, 4)
    window = rows + 2 * HALO
    flops = 2 * count * window * chans * rows
    down_slabs = (rows + HALO) // DOWN_SPAN
    end_slabs, own_slabs = 2 * HALO // SPREAD_SPAN, rows // SPREAD_SPAN
    slabs_scratch = pltpu.VMEM((window // READ_SPAN * chans, READ_SPAN), bf16)
    end_scratch = [
        pltpu.VMEM((end_slabs * chans, rows), bf16),
        pltpu.VMEM((end_slabs, count * chans, SPREAD_SPAN), bf16),
    ]
    own_scratch = [
        pltpu.VMEM((own_slabs * chans, rows), bf16),
        pltpu.VMEM((own_slabs, count * chans, SPREAD_SPAN), bf16),
    ]

    before = shifted(field[:, rows - HALO :], "space", 1)
    after = shifted(field[:, :HALO], "space", -1)
    grad_rows, spread_next = call(
        spread_kernel,
        [shape((chans, rows), f32), shape((chans, HALO), bf16)],
        [pltpu.VMEM((down_slabs * chans, coarse), bf16)],
        2 * kids * (rows + HALO) * chans * coarse,
        children,
        weight_down,
        grad_out,
    )
    first, slope, taken, to_next = call(
        first_kernel,
        [
            shape((chans, rows), bf16),
            shape((chans, rows), f32),
            shape((count * chans, rows), bf16),
            shape((2 * chans, HALO), bf16),
        ],
        [slabs_scratch],
        flops,
        info,
        offsets,
        weight_first,
        field,
        before,
        after,
        spread_next,
    )
    before = shifted(to_next, "space", 1)
    after = shifted(first[:, :HALO], "space", -1)
    second, d_second, grad_second, to_prev, to_next = call(
        second_kernel,
        [
            shape((chans, rows), bf16),
            shape((chans, rows), bf16),
            shape((chans, count * chans), f32),
            shape((2 * chans, HALO), bf16),
            shape((chans, HALO), bf16),
        ],
        [slabs_scratch, pltpu.VMEM((count * chans, rows), bf16)] + end_scratch,
        flops * 3 // 2,
        info,
        offsets,
        weight_second,
        first,
        before,
        after,
        field,
        grad_rows,
    )
    from_next = shifted(to_prev, "space", -1)
    from_prev = shifted(to_next, "space", 1)
    (own,) = call(
        own_kernel,
        [shape((chans, rows), f32)],
        own_scratch,
        flops // 2,
        offsets,
        weight_second,
        d_second,
    )
    coarse_out, d_first, grads = call(
        middle_kernel,
        [
            shape((coarse, wide), bf16),
            shape((chans, rows), bf16),
            shape((chans, 2 * count * chans + kids * wide), f32),
        ],
        [
            pltpu.VMEM((down_slabs * chans, DOWN_SPAN), bf16),
            pltpu.VMEM((kids * chans, coarse), bf16),
        ],
        2 * kids * (rows + HALO) * chans * coarse,
        info,
        children,
        weight_down,
        grad_out,
        second,
        from_next,
        from_prev,
        own,
        slope,
        taken,
        grad_second,
    )
    samples = lax.axis_size("dp")
    direct = samples == 4 and devices == 4
    scale = float(samples * devices * rows) ** (-0.5)
    me = lax.axis_index("dp")
    share = chans // samples

    def partner(value, step):
        return lax.ppermute(value, "dp", [(i, i ^ step) for i in range(samples)])

    def quarter(step):
        return lax.dynamic_slice_in_dim(grads, (me ^ step) * share, share, axis=0)

    if direct:
        sent = [quarter(s).astype(bf16) for s in range(1, samples)]
        got = [partner(v, s + 1) for s, v in enumerate(sent)]
    to_prev, to_next = call(
        ends_kernel,
        [shape((chans, HALO), bf16), shape((chans, HALO), bf16)],
        end_scratch,
        flops // 2,
        offsets,
        weight_first,
        d_first,
    )
    if direct:
        part = quarter(0) + sum(v.astype(f32) for v in got)
        sent = part.astype(bf16)
        got = [shifted(sent, "space", s) for s in range(1, devices)]
    after = shifted(to_prev, "space", -1)
    before = shifted(to_next, "space", 1)
    (own,) = call(
        own_kernel,
        [shape((chans, rows), f32)],
        own_scratch,
        flops // 2,
        offsets,
        weight_first,
        d_first,
    )
    if direct:
        terms = [v.astype(f32) for v in [sent] + got]
        part = (((terms[0] + terms[2]) + (terms[1] + terms[3])) * scale).astype(bf16)
        parts = [part] + [partner(part, s) for s in range(1, samples)]
        grads = jnp.zeros(grads.shape, bf16)
        for s, v in enumerate(parts):
            grads = lax.dynamic_update_slice_in_dim(grads, v, (me ^ s) * share, axis=0)
    else:
        grads = (lax.psum(grads, ("space", "dp")) * scale).astype(bf16)
    feature_grad, out_first, out_second, out_down = call(
        last_kernel,
        [
            shape((chans, rows), bf16),
            shape(weight_first.shape, bf16),
            shape(weight_second.shape, bf16),
            shape(weight_down.shape, bf16),
        ],
        [],
        1,
        info,
        own,
        d_second,
        before,
        after,
        grads,
    )
    return (coarse_out[None], feature_grad.T[None], out_first, out_second, out_down)


def solution(mesh):
    placed = (
        P(("groups", "dp"), "space", None),
        P(("groups", "dp"), None, "space"),
        P(("groups", "dp"), None, "space"),
        P(("groups", "dp"), "space"),
        P(),
        P(),
        P(),
        P(("groups", "dp"), "space", None),
    )
    return jax.shard_map(
        body,
        mesh=mesh,
        in_specs=placed,
        out_specs=(
            P(("groups", "dp"), "space", None),
            P(("groups", "dp"), "space", None),
            P("groups", None, None),
            P("groups", None, None),
            P("groups", None, None),
        ),
        check_vma=False,
    )
```

time: 1130 us -> 125 us (0.11)
  other arithmetic: 504 us -> 0.26 us
  local copies, waits for them, and re-layouts: 379 us -> 5.91 us
  waiting for transfers between devices: 133 us -> 17 us
  Pallas kernels: 0 us -> 75.9 us
  matrix products: 34.8 us -> 0 us
  starting transfers between devices: 53.5 us -> 23.6 us
  between operations: 15.9 us -> 1.56 us
    scatter-add x12 -> x0, other arithmetic: 473 us -> none  [the longest x6 455 us: conv_back(): total.at[offsets[begin:begin + 9].T.reshape(-1)]]
    gather x6 -> x0, local copies, waits for them, and re-layouts: 211 us -> none  [the longest x4 201 us: collect(): return jnp.take(padded, offsets.T, axis=0).reshape(rows, -1)]
    psum x1 -> x0, waiting for transfers between devices: 126 us -> none  [body(): summed = lax.psum((grad_first, grad_second, grad_down), ('space', 'dp'))]
    pallas_call x0 -> x8, Pallas kernels: none -> 75.9 us  [call(): pl.pallas_call(kernel, out_shape=outs, in_specs=[smem if a.shape == (1, 4...]
    reshape x11 -> x0, local copies, waits for them, and re-layouts: 66.3 us -> none  [the longest x6 64.2 us: conv_back(): terms.reshape(-1, chans)]
    dot_general x6 -> x0, local copies, waits for them, and re-layouts: 61.2 us -> none  [conv_back(): jnp.einsum('ro,kio->rki', d_pre, weights[begin:begin + 9], preferred_elem...]
    dot_general x13 -> x0, matrix products: 34.8 us -> none  [the longest x6 15.3 us: conv_back(): jnp.einsum('ro,kio->rki', d_pre, weights[begin:begin + 9], preferred_elem...]
    select_n x4 -> x0, local copies, waits for them, and re-layouts: 31.4 us -> none  [the longest x3 31.3 us: collect(): return jnp.take(padded, offsets.T, axis=0).reshape(rows, -1)]
  transfers between devices with their start and end apart: 11 -> 17, of which waited for: 4 -> 6; matrix products, arithmetic and copies ran while one was open for 48% -> 0% of each run, Pallas kernels for 0% -> 23%
where the time goes in v2:
time: 125 us; the launch traced here: 124 us
  Pallas kernels  75.9 us (61%)
  starting transfers between devices  23.6 us (19%)
  waiting for transfers between devices  17 us (14%)
  local copies, waits for them, and re-layouts  5.91 us (5%)
  between operations  1.56 us (1%)
    pallas_call x8, Pallas kernels, call(): pl.pallas_call(kernel, out_shape=outs, in_specs=[smem if a.shape == (1, 4...  75.9 us
    ppermute x11, starting transfers between devices, shifted(): lax.ppermute(value, axis, [(i, (i + steps) % count) for i in range(count)])  20.1 us
    ppermute x6, waiting for transfers between devices, partner(): return lax.ppermute(value, 'dp', [(i, i ^ step) for i in range(samples)])  13.3 us
    unnamed x26, local copies, waits for them, and re-layouts  4.87 us
    ppermute x11, waiting for transfers between devices, shifted(): lax.ppermute(value, axis, [(i, (i + steps) % count) for i in range(count)])  3.65 us
    ppermute x6, starting transfers between devices, partner(): return lax.ppermute(value, 'dp', [(i, i ^ step) for i in range(samples)])  3.56 us
  transfers between devices with their start and end apart: 17, of which 6 were waited for; matrix products, arithmetic and copies ran while one was open for 0% of the time, Pallas kernels for 23%

profile of v2, /device:TPU:0, one launch (start us, length us, event | category | flops | bytes accessed | tf_op | source)
XLA Modules:
  0.0 124.3 jit_solution(3942740111075495907)
XLA Ops:
  0.6 0.9 fusion
  1.5 3.1 %collective-permute-start = (bf16[64,512]{1,0:T(8,128)(2,1)S(1)}, bf16[64,512]{1,0:T(8,128)(2,1)S(1)}, u32[]{:S(2)}, u32[]{:S(2)}) collective-permute-start(bf16[64,512]{1,0:T(8,128)(2,1)S(1)} %get-tuple-element.51), channel_id=1, source_target_pairs={{0,4},{4,8},{8,12},{12,0},{1,5},{5,9},{9,13},{13,1},{2,6},{6,10},{... | collective-permute-start | bytes 196616 | tf_op jit(solution)/shard_map/ppermute | solution.py:307
  4.6 2.1 %collective-permute-start.1 = (bf16[64,512]{1,0:T(8,128)(2,1)S(1)}, bf16[64,512]{1,0:T(8,128)(2,1)S(1)}, u32[]{:S(2)}, u32[]{:S(2)}) collective-permute-start(bf16[64,512]{1,0:T(8,128)(2,1)S(1)} %get-tuple-element.50), channel_id=1, source_target_pairs={{0,12},{4,0},{8,4},{12,8},{1,13},{5,1},{9,5},{13,9},{2,14},{6,2},{... | collective-permute-start | bytes 196616 | tf_op jit(solution)/shard_map/ppermute | solution.py:307
  7.3 0.1 add_bitcast_fusion.info_ref
  7.4 0.9 copy-done.1
  8.3 0.9 copy-done.3
  9.2 0.7 copy-done.6
  9.9 1.6 %shard_map.119 = (f32[64,1536]{1,0:T(8,128)S(1)}, bf16[64,512]{1,0:T(8,128)(2,1)S(1)}) custom-call(s32[8,384]{1,0:T(8,128)S(1)} %bitcast.24, bf16[8,64,128]{2,1,0:T(8,128)(2,1)S(1)} %copy-done.1, bf16[384,128]{1,0:T(8,128)(2,1)S(1)} %bitcast.19), custom_call_target="tpu_custom_call" | custom-call | flops 805306368 | bytes 1048576 | tf_op jit(solution)/shard_map/pallas_call | solution.py:294
  11.5 0.0 collective-permute-done.before_ref
  11.5 0.0 collective-permute-done.1.after_ref
  11.6 0.0 copy-start.8
  11.6 16.6 %shard_map.120 = (bf16[64,1536]{1,0:T(8,128)(2,1)S(1)}, f32[64,1536]{1,0:T(8,128)S(1)}, bf16[1728,1536]{1,0:T(8,128)(2,1)S(1)}, bf16[128,512]{1,0:T(8,128)(2,1)S(1)}) custom-call(s32[1,4]{1,0:T(1,128)S(1)} %add_bitcast_fusion.info_ref, s32[27,1,1536]{2,1,0:T(1,128)S(1)} %bitcast.26, bf16[27,64,64]{2,1,0:T(8,128)(2,1)S(1)} %copy-done.9, ...), custom_call_target="tpu_custom_call" | custom-call | flops 13589544960 | bytes 1048576 | tf_op jit(solution)/shard_map/pallas_call | solution.py:294
  28.2 2.3 %copy-done = bf16[1728,1536]{1,0:T(8,128)(2,1)} copy-done((bf16[1728,1536]{1,0:T(8,128)(2,1)}, bf16[1728,1536]{1,0:T(8,128)(2,1)S(1)}, u32[]{:S(2)}) %copy-start) | copy-done | bytes 5308440
  30.5 0.0 collective-permute-start.2
  30.5 3.8 %collective-permute-start.3 = (bf16[64,512]{1,0:T(8,128)(2,1)S(1)}, bf16[64,512]{1,0:T(8,128)(2,1)S(1)}, u32[]{:S(2)}, u32[]{:S(2)}) collective-permute-start(bf16[64,512]{1,0:T(8,128)(2,1)S(1)} %slice.11), channel_id=1, source_target_pairs={{0,12},{4,0},{8,4},{12,8},{1,13},{5,1},{9,5},{13,9},{2,14},{6,2},{... | collective-permute-start | bytes 196616 | tf_op jit(solution)/shard_map/ppermute | solution.py:307
  34.4 2.6 %collective-permute-done.3.after_ref = bf16[64,512]{1,0:T(8,128)(2,1)S(1)} collective-permute-done((bf16[64,512]{1,0:T(8,128)(2,1)S(1)}, bf16[64,512]{1,0:T(8,128)(2,1)S(1)}, u32[]{:S(2)}, u32[]{:S(2)}) %collective-permute-start.3) | collective-permute-done | bytes 65568 | tf_op jit(solution)/shard_map/ppermute | solution.py:307
  36.9 1.0 collective-permute-done.2.before_ref
  38.0 24.7 %shard_map.121 = (bf16[64,1536]{1,0:T(8,128)(2,1)S(1)}, bf16[64,1536]{1,0:T(8,128)(2,1)S(1)}, f32[64,1728]{1,0:T(8,128)S(1)}, bf16[128,512]{1,0:T(8,128)(2,1)S(1)}, bf16[64,512]{1,0:T(8,128)(2,1)S(1)}) custom-call(s32[1,4]{1,0:T(1,128)S(1)} %add_bitcast_fusion.info_ref, s32[27,1,1536]{2,1,0:T(1,128)S(1)} %bitcast.27, bf16[27,64,64]{2,1,0:T(8,128)(2,1)S(1)} %copy-done.8, ...), custom_call_target="tpu_custom_call" | custom-call | flops 20384317440 | bytes 1048576 | tf_op jit(solution)/shard_map/pallas_call | solution.py:294
  62.7 2.5 %collective-permute-start.4 = (bf16[128,512]{1,0:T(8,128)(2,1)S(1)}, bf16[128,512]{1,0:T(8,128)(2,1)S(1)}, u32[]{:S(2)}, u32[]{:S(2)}) collective-permute-start(bf16[128,512]{1,0:T(8,128)(2,1)S(1)} %get-tuple-element.30), channel_id=1, source_target_pairs={{0,12},{4,0},{8,4},{12,8},{1,13},{5,1},{9,5},{13,9},{2,14},{6,2},{... | collective-permute-start | bytes 393224 | tf_op jit(solution)/shard_map/ppermute | solution.py:307
  65.2 0.0 collective-permute-start.5
  65.2 0.0 copy-start.4
  65.2 0.0 copy-start.7
  65.2 10.1 %shard_map.122.rows_ref = f32[64,1536]{1,0:T(8,128)S(1)} custom-call(s32[27,1,1536]{2,1,0:T(1,128)S(1)} %bitcast.28, bf16[27,64,64]{2,1,0:T(8,128)(2,1)S(1)} %copy-done.8, bf16[64,1536]{1,0:T(8,128)(2,1)S(1)} %get-tuple-element.32.grad_ref.d_second_ref), custom_call_target="tpu_custom_call" | custom-call | flops 6794772480 | bytes 1048576 | tf_op jit(solution)/shard_map/pallas_call | solution.py:294
  75.3 0.0 collective-permute-done.4.from_next_ref
  75.3 4.1 %shard_map.123 = (bf16[384,128]{1,0:T(8,128)(2,1)}, bf16[64,1536]{1,0:T(8,128)(2,1)S(1)}, f32[64,4480]{1,0:T(8,128)S(1)}) custom-call(s32[1,4]{1,0:T(1,128)S(1)} %add_bitcast_fusion.info_ref, s32[8,384]{1,0:T(8,128)S(1)} %bitcast.25, bf16[8,64,128]{2,1,0:T(8,128)(2,1)S(1)} %copy-done.2, bf16[384,128]{1,0:T(8,128)(2,1)S(1)} %bitcast.20, ...), custom_call_target="tpu_custom_call" | custom-call | flops 805306368 | bytes 1048576 | tf_op jit(solution)/shard_map/pallas_call | solution.py:294
  79.4 0.1 dynamic-slice_convert_fusion.2
  79.5 0.1 collective-permute-start.10
  79.6 1.8 %collective-permute-start.8 = (bf16[16,4480]{1,0:T(8,128)(2,1)S(1)}, bf16[16,4480]{1,0:T(8,128)(2,1)S(1)}, u32[]{:S(2)}, u32[]{:S(2)}) collective-permute-start(bf16[16,4480]{1,0:T(8,128)(2,1)S(1)} %get-tuple-element.47), channel_id=1, source_target_pairs={{0,1},{1,0},{2,3},{3,2},{4,5},{5,4},{6,7},{7,6},{8,9},{9,8},{10,11... | collective-permute-start | bytes 430088 | tf_op jit(solution)/shard_map/ppermute | solution.py:439
  81.3 0.4 collective-permute-start.9
  81.7 3.7 %collective-permute-done.10 = bf16[16,4480]{1,0:T(8,128)(2,1)S(1)} collective-permute-done((bf16[16,4480]{1,0:T(8,128)(2,1)S(1)}, bf16[16,4480]{1,0:T(8,128)(2,1)S(1)}, u32[]{:S(2)}, u32[]{:S(2)}) %collective-permute-start.10) | collective-permute-done | bytes 143392 | tf_op jit(solution)/shard_map/ppermute | solution.py:439
  85.4 3.3 %collective-permute-done.9 = bf16[16,4480]{1,0:T(8,128)(2,1)S(1)} collective-permute-done((bf16[16,4480]{1,0:T(8,128)(2,1)S(1)}, bf16[16,4480]{1,0:T(8,128)(2,1)S(1)}, u32[]{:S(2)}, u32[]{:S(2)}) %collective-permute-start.9) | collective-permute-done | bytes 143392 | tf_op jit(solution)/shard_map/ppermute | solution.py:439
  88.7 0.1 add_convert_fusion
  88.8 0.9 collective-permute-start.11
  89.6 3.5 %collective-permute-start.12 = (bf16[16,4480]{1,0:T(8,128)(2,1)S(1)}, bf16[16,4480]{1,0:T(8,128)(2,1)S(1)}, u32[]{:S(2)}, u32[]{:S(2)}) collective-permute-start(bf16[16,4480]{1,0:T(8,128)(2,1)S(1)} %add_convert_fusion), channel_id=1, source_target_pairs={{0,4},{4,8},{8,12},{12,0},{1,5},{5,9},{9,13},{13,1},{2,6},{6,10},{... | collective-permute-start | bytes 430088 | tf_op jit(solution)/shard_map/ppermute | solution.py:307
  93.2 0.3 collective-permute-start.13
  93.5 10.1 %shard_map.124.own_ref = f32[64,1536]{1,0:T(8,128)S(1)} custom-call(s32[27,1,1536]{2,1,0:T(1,128)S(1)} %bitcast.29, bf16[27,64,64]{2,1,0:T(8,128)(2,1)S(1)} %copy-done.9, bf16[64,1536]{1,0:T(8,128)(2,1)S(1)} %get-tuple-element.37.grad_ref), custom_call_target="tpu_custom_call" | custom-call | flops 6794772480 | bytes 1048576 | tf_op jit(solution)/shard_map/pallas_call | solution.py:294
  103.6 0.0 collective-permute-done.13
  103.6 0.1 constant_dynamic-update-slice_fusion.3
  103.7 0.1 collective-permute-start.14
  103.8 6.9 %shard_map.125 = (bf16[64,512]{1,0:T(8,128)(2,1)S(1)}, bf16[64,512]{1,0:T(8,128)(2,1)S(1)}) custom-call(s32[27,1,1536]{2,1,0:T(1,128)S(1)} %bitcast.30, bf16[27,64,64]{2,1,0:T(8,128)(2,1)S(1)} %copy-done.9, bf16[64,1536]{1,0:T(8,128)(2,1)S(1)} %get-tuple-element.37.grad_ref), custom_call_target="tpu_custom_call" | custom-call | flops 6794772480 | bytes 1048576 | tf_op jit(solution)/shard_map/pallas_call | solution.py:294
  110.7 1.8 %collective-permute-start.6 = (bf16[64,512]{1,0:T(8,128)(2,1)S(1)}, bf16[64,512]{1,0:T(8,128)(2,1)S(1)}, u32[]{:S(2)}, u32[]{:S(2)}) collective-permute-start(bf16[64,512]{1,0:T(8,128)(2,1)S(1)} %get-tuple-element.38), channel_id=1, source_target_pairs={{0,4},{4,8},{8,12},{12,0},{1,5},{5,9},{9,13},{13,1},{2,6},{6,10},{... | collective-permute-start | bytes 196616 | tf_op jit(solution)/shard_map/ppermute | solution.py:307
  112.5 2.1 %collective-permute-start.7 = (bf16[64,512]{1,0:T(8,128)(2,1)S(1)}, bf16[64,512]{1,0:T(8,128)(2,1)S(1)}, u32[]{:S(2)}, u32[]{:S(2)}) collective-permute-start(bf16[64,512]{1,0:T(8,128)(2,1)S(1)} %get-tuple-element.39), channel_id=1, source_target_pairs={{0,12},{4,0},{8,4},{12,8},{1,13},{5,1},{9,5},{13,9},{2,14},{6,2},{... | collective-permute-start | bytes 196616 | tf_op jit(solution)/shard_map/ppermute | solution.py:307
  114.6 0.1 collective-permute-start.15
  114.7 1.2 collective-permute-start.16
  115.9 5.3 %collective-permute-done.15 = bf16[16,4480]{1,0:T(8,128)(2,1)S(1)} collective-permute-done((bf16[16,4480]{1,0:T(8,128)(2,1)S(1)}, bf16[16,4480]{1,0:T(8,128)(2,1)S(1)}, u32[]{:S(2)}, u32[]{:S(2)}) %collective-permute-start.15) | collective-permute-done | bytes 143392 | tf_op jit(solution)/shard_map/ppermute | solution.py:439
  121.3 1.0 collective-permute-done.16
  122.3 0.0 collective-permute-done.7.after_ref
  122.3 2.0 %shard_map.126 = (bf16[64,1536]{1,0:T(8,128)(2,1)}, bf16[27,64,64]{2,1,0:T(8,128)(2,1)}, bf16[27,64,64]{2,1,0:T(8,128)(2,1)}, bf16[8,64,128]{2,1,0:T(8,128)(2,1)}) custom-call(s32[1,4]{1,0:T(1,128)S(1)} %add_bitcast_fusion.info_ref, f32[64,1536]{1,0:T(8,128)S(1)} %shard_map.124.own_ref, bf16[64,1536]{1,0:T(8,128)(2,1)S(1)} %get-tuple-element.32.grad_ref.d_second_ref, ...), custom_call_target="tpu_custom_call" | custom-call | flops 1 | bytes 1048576 | tf_op jit(solution)/shard_map/pallas_call | solution.py:294
  (31 shorter events, 0.2 us)
Async XLA Ops:
  1.5 10.0 %collective-permute-start = (bf16[64,512]{1,0:T(8,128)(2,1)S(1)}, bf16[64,512]{1,0:T(8,128)(2,1)S(1)}, u32[]{:S(2)}, u32[]{:S(2)}) collective-permute-start(bf16[64,512]{1,0:T(8,128)(2,1)S(1)} %get-tuple-element.51), channel_id=1, source_target_pairs={{0,4},{4,8},{8,12},{12,0},{1,5},{5,9},{9,13},{13,1},{2,6},{6,10},{... | collective-permute-start | bytes 196616 | tf_op jit(solution)/shard_map/ppermute | solution.py:307
  4.6 7.0 %collective-permute-start.1 = (bf16[64,512]{1,0:T(8,128)(2,1)S(1)}, bf16[64,512]{1,0:T(8,128)(2,1)S(1)}, u32[]{:S(2)}, u32[]{:S(2)}) collective-permute-start(bf16[64,512]{1,0:T(8,128)(2,1)S(1)} %get-tuple-element.50), channel_id=1, source_target_pairs={{0,12},{4,0},{8,4},{12,8},{1,13},{5,1},{9,5},{13,9},{2,14},{6,2},{... | collective-permute-start | bytes 196616 | tf_op jit(solution)/shard_map/ppermute | solution.py:307
  7.4 0.9 copy-start.1
  8.3 0.9 copy-start.3
  9.2 0.7 copy-start.6
  9.9 1.6 %copy-start.5 = (bf16[1,1536,64]{1,2,0:T(8,128)(2,1)S(1)}, bf16[1,1536,64]{1,2,0:T(8,128)(2,1)}, u32[]{:S(2)}) copy-start(bf16[1,1536,64]{1,2,0:T(8,128)(2,1)} %param.8) | copy-start | bytes 589828
  9.9 1.6 %copy-start.9 = (bf16[27,64,64]{2,1,0:T(8,128)(2,1)S(1)}, bf16[27,64,64]{2,1,0:T(8,128)(2,1)}, u32[]{:S(2)}) copy-start(bf16[27,64,64]{2,1,0:T(8,128)(2,1)} %weight_ref.9) | copy-start | bytes 663556
  9.9 1.6 %copy-start.10 = (s32[1,27,1536]{2,0,1:T(1,128)S(1)}, s32[1,27,1536]{2,0,1:T(1,128)}, u32[]{:S(2)}) copy-start(s32[1,27,1536]{2,0,1:T(1,128)} %param.9) | copy-start | bytes 497668
  11.6 26.4 %copy-start.8 = (bf16[27,64,64]{2,1,0:T(8,128)(2,1)S(1)}, bf16[27,64,64]{2,1,0:T(8,128)(2,1)}, u32[]{:S(2)}) copy-start(bf16[27,64,64]{2,1,0:T(8,128)(2,1)} %weight_ref.7) | copy-start | bytes 663556
  28.2 2.3 %copy-start = (bf16[1728,1536]{1,0:T(8,128)(2,1)}, bf16[1728,1536]{1,0:T(8,128)(2,1)S(1)}, u32[]{:S(2)}) copy-start(bf16[1728,1536]{1,0:T(8,128)(2,1)S(1)} %get-tuple-element.34.taken_ref) | copy-start | bytes 15925252
  30.5 7.5 %collective-permute-start.2 = (bf16[128,512]{1,0:T(8,128)(2,1)S(1)}, bf16[128,512]{1,0:T(8,128)(2,1)S(1)}, u32[]{:S(2)}, u32[]{:S(2)}) collective-permute-start(bf16[128,512]{1,0:T(8,128)(2,1)S(1)} %get-tuple-element.27), channel_id=1, source_target_pairs={{0,4},{4,8},{8,12},{12,0},{1,5},{5,9},{9,13},{13,1},{2,6},{6,10},{... | collective-permute-start | bytes 393224 | tf_op jit(solution)/shard_map/ppermute | solution.py:307
  30.5 6.4 %collective-permute-start.3 = (bf16[64,512]{1,0:T(8,128)(2,1)S(1)}, bf16[64,512]{1,0:T(8,128)(2,1)S(1)}, u32[]{:S(2)}, u32[]{:S(2)}) collective-permute-start(bf16[64,512]{1,0:T(8,128)(2,1)S(1)} %slice.11), channel_id=1, source_target_pairs={{0,12},{4,0},{8,4},{12,8},{1,13},{5,1},{9,5},{13,9},{2,14},{6,2},{... | collective-permute-start | bytes 196616 | tf_op jit(solution)/shard_map/ppermute | solution.py:307
  62.7 12.6 %collective-permute-start.4 = (bf16[128,512]{1,0:T(8,128)(2,1)S(1)}, bf16[128,512]{1,0:T(8,128)(2,1)S(1)}, u32[]{:S(2)}, u32[]{:S(2)}) collective-permute-start(bf16[128,512]{1,0:T(8,128)(2,1)S(1)} %get-tuple-element.30), channel_id=1, source_target_pairs={{0,12},{4,0},{8,4},{12,8},{1,13},{5,1},{9,5},{13,9},{2,14},{6,2},{... | collective-permute-start | bytes 393224 | tf_op jit(solution)/shard_map/ppermute | solution.py:307
  65.2 10.1 %collective-permute-start.5 = (bf16[64,512]{1,0:T(8,128)(2,1)S(1)}, bf16[64,512]{1,0:T(8,128)(2,1)S(1)}, u32[]{:S(2)}, u32[]{:S(2)}) collective-permute-start(bf16[64,512]{1,0:T(8,128)(2,1)S(1)} %get-tuple-element.31), channel_id=1, source_target_pairs={{0,4},{4,8},{8,12},{12,0},{1,5},{5,9},{9,13},{13,1},{2,6},{6,10},{... | collective-permute-start | bytes 196616 | tf_op jit(solution)/shard_map/ppermute | solution.py:307
  65.2 10.1 %slice-start = ((s8[5308416]{0:T(1024)(128)(4,1)}), s8[4194304]{0:T(1024)(128)(4,1)S(1)}, s32[]{:S(2)}) async-start(s8[5308416]{0:T(1024)(128)(4,1)} %bitcast.17), calls=%async_computation | async-start | bytes 8388608
  65.2 10.1 %slice-start.1 = ((s8[5308416]{0:T(1024)(128)(4,1)}), s8[1114112]{0:T(1024)(128)(4,1)S(1)}, s32[]{:S(2)}) async-start(s8[5308416]{0:T(1024)(128)(4,1)} %bitcast.17), calls=%async_computation.1 | async-start | bytes 2228224
  65.2 10.1 %copy-start.2 = (bf16[8,64,128]{2,1,0:T(8,128)(2,1)S(1)}, bf16[8,64,128]{2,1,0:T(8,128)(2,1)}, u32[]{:S(2)}) copy-start(bf16[8,64,128]{2,1,0:T(8,128)(2,1)} %down_ref.3) | copy-start | bytes 393220
  65.2 10.2 %copy-start.4 = (bf16[1,384,128]{2,1,0:T(8,128)(2,1)S(1)}, bf16[1,384,128]{2,1,0:T(8,128)(2,1)}, u32[]{:S(2)}) copy-start(bf16[1,384,128]{2,1,0:T(8,128)(2,1)} %param.15) | copy-start | bytes 294916
  65.2 10.1 %copy-start.7 = (s32[1,8,384]{2,1,0:T(8,128)S(1)}, s32[1,8,384]{2,1,0:T(8,128)}, u32[]{:S(2)}) copy-start(s32[1,8,384]{2,1,0:T(8,128)} %param.10) | copy-start | bytes 36868
  79.5 5.9 %collective-permute-start.10 = (bf16[16,4480]{1,0:T(8,128)(2,1)S(1)}, bf16[16,4480]{1,0:T(8,128)(2,1)S(1)}, u32[]{:S(2)}, u32[]{:S(2)}) collective-permute-start(bf16[16,4480]{1,0:T(8,128)(2,1)S(1)} %get-tuple-element.48), channel_id=1, source_target_pairs={{0,3},{1,2},{2,1},{3,0},{4,7},{5,6},{6,5},{7,4},{8,11},{9,10},{10,... | collective-permute-start | bytes 430088 | tf_op jit(solution)/shard_map/ppermute | solution.py:439
  79.6 5.8 %collective-permute-start.8 = (bf16[16,4480]{1,0:T(8,128)(2,1)S(1)}, bf16[16,4480]{1,0:T(8,128)(2,1)S(1)}, u32[]{:S(2)}, u32[]{:S(2)}) collective-permute-start(bf16[16,4480]{1,0:T(8,128)(2,1)S(1)} %get-tuple-element.47), channel_id=1, source_target_pairs={{0,1},{1,0},{2,3},{3,2},{4,5},{5,4},{6,7},{7,6},{8,9},{9,8},{10,11... | collective-permute-start | bytes 430088 | tf_op jit(solution)/shard_map/ppermute | solution.py:439
  81.3 7.4 %collective-permute-start.9 = (bf16[16,4480]{1,0:T(8,128)(2,1)S(1)}, bf16[16,4480]{1,0:T(8,128)(2,1)S(1)}, u32[]{:S(2)}, u32[]{:S(2)}) collective-permute-start(bf16[16,4480]{1,0:T(8,128)(2,1)S(1)} %get-tuple-element.49), channel_id=1, source_target_pairs={{0,2},{1,3},{2,0},{3,1},{4,6},{5,7},{6,4},{7,5},{8,10},{9,11},{10,... | collective-permute-start | bytes 430088 | tf_op jit(solution)/shard_map/ppermute | solution.py:439
  88.8 14.8 %collective-permute-start.11 = (bf16[16,4480]{1,0:T(8,128)(2,1)S(1)}, bf16[16,4480]{1,0:T(8,128)(2,1)S(1)}, u32[]{:S(2)}, u32[]{:S(2)}) collective-permute-start(bf16[16,4480]{1,0:T(8,128)(2,1)S(1)} %add_convert_fusion), channel_id=1, source_target_pairs={{0,8},{4,12},{8,0},{12,4},{1,9},{5,13},{9,1},{13,5},{2,10},{6,14},... | collective-permute-start | bytes 430088 | tf_op jit(solution)/shard_map/ppermute | solution.py:307
  89.6 13.9 %collective-permute-start.12 = (bf16[16,4480]{1,0:T(8,128)(2,1)S(1)}, bf16[16,4480]{1,0:T(8,128)(2,1)S(1)}, u32[]{:S(2)}, u32[]{:S(2)}) collective-permute-start(bf16[16,4480]{1,0:T(8,128)(2,1)S(1)} %add_convert_fusion), channel_id=1, source_target_pairs={{0,4},{4,8},{8,12},{12,0},{1,5},{5,9},{9,13},{13,1},{2,6},{6,10},{... | collective-permute-start | bytes 430088 | tf_op jit(solution)/shard_map/ppermute | solution.py:307
  93.2 10.4 %collective-permute-start.13 = (bf16[16,4480]{1,0:T(8,128)(2,1)S(1)}, bf16[16,4480]{1,0:T(8,128)(2,1)S(1)}, u32[]{:S(2)}, u32[]{:S(2)}) collective-permute-start(bf16[16,4480]{1,0:T(8,128)(2,1)S(1)} %add_convert_fusion), channel_id=1, source_target_pairs={{0,12},{4,0},{8,4},{12,8},{1,13},{5,1},{9,5},{13,9},{2,14},{6,2},{... | collective-permute-start | bytes 430088 | tf_op jit(solution)/shard_map/ppermute | solution.py:307
  103.7 12.2 %collective-permute-start.14 = (bf16[16,4480]{1,0:T(8,128)(2,1)S(1)}, bf16[16,4480]{1,0:T(8,128)(2,1)S(1)}, u32[]{:S(2)}, u32[]{:S(2)}) collective-permute-start(bf16[16,4480]{1,0:T(8,128)(2,1)S(1)} %get-tuple-element.46), channel_id=1, source_target_pairs={{0,1},{1,0},{2,3},{3,2},{4,5},{5,4},{6,7},{7,6},{8,9},{9,8},{10,11... | collective-permute-start | bytes 430088 | tf_op jit(solution)/shard_map/ppermute | solution.py:439
  110.7 11.5 %collective-permute-start.6 = (bf16[64,512]{1,0:T(8,128)(2,1)S(1)}, bf16[64,512]{1,0:T(8,128)(2,1)S(1)}, u32[]{:S(2)}, u32[]{:S(2)}) collective-permute-start(bf16[64,512]{1,0:T(8,128)(2,1)S(1)} %get-tuple-element.38), channel_id=1, source_target_pairs={{0,4},{4,8},{8,12},{12,0},{1,5},{5,9},{9,13},{13,1},{2,6},{6,10},{... | collective-permute-start | bytes 196616 | tf_op jit(solution)/shard_map/ppermute | solution.py:307
  112.5 9.8 %collective-permute-start.7 = (bf16[64,512]{1,0:T(8,128)(2,1)S(1)}, bf16[64,512]{1,0:T(8,128)(2,1)S(1)}, u32[]{:S(2)}, u32[]{:S(2)}) collective-permute-start(bf16[64,512]{1,0:T(8,128)(2,1)S(1)} %get-tuple-element.39), channel_id=1, source_target_pairs={{0,12},{4,0},{8,4},{12,8},{1,13},{5,1},{9,5},{13,9},{2,14},{6,2},{... | collective-permute-start | bytes 196616 | tf_op jit(solution)/shard_map/ppermute | solution.py:307
  114.6 6.6 %collective-permute-start.15 = (bf16[16,4480]{1,0:T(8,128)(2,1)S(1)}, bf16[16,4480]{1,0:T(8,128)(2,1)S(1)}, u32[]{:S(2)}, u32[]{:S(2)}) collective-permute-start(bf16[16,4480]{1,0:T(8,128)(2,1)S(1)} %get-tuple-element.46), channel_id=1, source_target_pairs={{0,2},{1,3},{2,0},{3,1},{4,6},{5,7},{6,4},{7,5},{8,10},{9,11},{10,... | collective-permute-start | bytes 430088 | tf_op jit(solution)/shard_map/ppermute | solution.py:439
  114.7 7.6 %collective-permute-start.16 = (bf16[16,4480]{1,0:T(8,128)(2,1)S(1)}, bf16[16,4480]{1,0:T(8,128)(2,1)S(1)}, u32[]{:S(2)}, u32[]{:S(2)}) collective-permute-start(bf16[16,4480]{1,0:T(8,128)(2,1)S(1)} %get-tuple-element.46), channel_id=1, source_target_pairs={{0,3},{1,2},{2,1},{3,0},{4,7},{5,6},{6,5},{7,4},{8,11},{9,10},{10,... | collective-permute-start | bytes 430088 | tf_op jit(solution)/shard_map/ppermute | solution.py:439
